TPU v7x, 32 devices: a whole 2x2x4 slice. The times are simulated.
32 devices in a mesh: tm: 8 (over z, x), fiber: 4 (over y, core).
Axes of the slice: x: 2, y: 2, z: 4, core: 2. Of those that a mesh axis runs over, the one named last changes fastest.
Arguments:
- signal: float32 [128, 4096], P('fiber', 'tm'), may hold values from -6 to 6
- encode_weight: float32 [64, 9], replicated, may hold values from -2 to 2
- encode_bias: float32 [64], replicated, may hold values from -3 to 3
- dilated_weight: float32 [6, 6, 64, 64], replicated, may hold values from -0.3125 to 0.3125
- dilated_bias: float32 [6, 64], replicated, may hold values from -3 to 3
- decode_weight: float32 [9, 64], replicated, may hold values from -0.5 to 0.5
Outputs:
- recon: float32 [128, 4096], P('fiber', 'tm')
- tile_error: float32 [8, 32], P('fiber', 'tm')
All inputs are finite; a program needn't handle non-finite values.
Results may differ from a plain program's by a relative error of at most 0.0001.
Values sent between devices are 32-bit elements; how exact they have to be, the bound alone decides.
No kernel may reach another device: no remote copies, remote signals or barrier semaphores. Data moves between devices by JAX's collectives and lax.ppermute only.
A program may use at most 64 MiB of HBM per device.

v0:
```python
import jax
import jax.numpy as jnp
from jax import lax
from jax.experimental import pallas as pl
from jax.experimental.pallas import tpu as pltpu
from jax.sharding import PartitionSpec as P

LAYERS = 6
F = 64
TILE_C = 16
TILE_T = 128
CB = 16
HB = 256
HH = 64
ROWS = HH + HB
PAIRS = (CB + 2 * LAYERS + 2) // 2
KEPT = (0, 0, 0, 0, 0, 16, 48)
HIST = 256
EDGE = 16
BF = jnp.bfloat16
F32 = jnp.float32


def split(x):
    hi = x.astype(BF)
    return hi, (x - hi.astype(F32)).astype(BF)


def from_behind(block, axis, distance):
    devices = range(lax.axis_size(axis))
    route = [(i - distance, i) for i in devices if i - distance in devices]
    return lax.ppermute(block, axis, route)


def prepare(ew_ref, dw_ref, de_ref, enc_ref, dil_ref, dec_ref, wide):
    ew = ew_ref[...]
    k = lax.broadcasted_iota(jnp.int32, (9, 256), 0)
    lane = lax.broadcasted_iota(jnp.int32, (9, 256), 1)
    base = []
    for j in range(4):
        pick = (lane // F == k % 3) & (lane % F == 3 + 2 * j + k // 3)
        base.append(
            jnp.dot(ew, pick.astype(F32), precision=lax.Precision.HIGHEST,
                    preferred_element_type=F32)
        )
    base = jnp.concatenate(base, 0).T
    none = jnp.zeros((F, 256), F32)
    for g in range(8):
        parts = []
        for b in range(3):
            piece = base[b * F : b * F + 16]
            if g < 7:
                rows = [none[: 8 * g], piece, none[: F - 16 - 8 * g]]
            else:
                rows = [none[: F - 8], piece[:8]]
            parts += [r for r in rows if r.shape[0]]
        parts.append(none)
        hi, lo = split(jnp.concatenate(parts, 0))
        enc_ref[g, 0:256] = hi
        enc_ref[g, 256:512] = hi
        enc_ref[g, 512:768] = lo
    zero = jnp.zeros((F, F), F32)
    for layer in range(LAYERS):
        odd = layer % 2
        ins = (1, 0, 3, 2) if odd else (0, 1, 2, 3)
        outs = (1, 2) if odd else (2, 1)
        for lag in range(2):
            for n, co in enumerate(outs):
                cols = [
                    dw_ref[layer, 2 * (ci - co + 1) + lag] * 0.5 if 0 <= ci - co + 1 <= 2 else zero
                    for ci in ins
                ]
                wide[pl.ds((2 * lag + n) * F, F), :] = jnp.concatenate(cols, 1)
        hi, lo = split(wide[...].T)
        dil_ref[layer, 0:256] = hi
        dil_ref[layer, 256:512] = hi
        dil_ref[layer, 512:768] = lo
    for q in range(9):
        wide[...] = jnp.zeros((256, 256), F32)
        for s in range(2):
            c = 2 * q + s
            for a in range(3):
                p = 2 * c + a - 1
                if 0 <= p < 2 * CB:
                    for b, at in enumerate((0, 32, 128)):
                        wide[at + p : at + p + 1, s * F : s * F + F] = de_ref[3 * a + b : 3 * a + b + 1, :]
        hi, lo = split(wide[:, 0:128].T)
        dec_ref[0, q * 128 : q * 128 + 128] = hi
        dec_ref[1, q * 128 : q * 128 + 128] = lo


def score(sig_ref, hist_ref, low_ref, high_ref, eb_ref, db_ref, enc_ref, dil_ref, dec_ref,
          recon_ref, err_ref, st, hid, top, low, mask, wide):
    first = lax.axis_index("fiber") == 0
    last = lax.axis_index("fiber") == lax.axis_size("fiber") - 1
    m_low = jnp.where(first, 0.0, 1.0).astype(F32)
    m_high = jnp.where(last, 0.0, 1.0).astype(F32)
    m_time = jnp.where(lax.axis_index("tm") == 0, 0.0, 1.0).astype(F32)
    pair = lax.broadcasted_iota(jnp.int32, (16, 128), 0)
    lane = lax.broadcasted_iota(jnp.int32, (16, 128), 1)
    for layer in range(LAYERS + 1):
        second = lane // F if layer % 2 == 0 else 1 - lane // F
        c = layer - LAYERS + 2 * pair + second
        mask[layer] = jnp.where(c < 0, m_low, jnp.where(c >= CB, m_high, 1.0))
    own = jnp.concatenate([hist_ref[...], sig_ref[...]], 1)
    s = jnp.concatenate([low_ref[...], own, high_ref[...]], 0)
    both = jnp.concatenate([s, pltpu.roll(s, 1, 1)], 0)
    for n in range((HIST + 2 * HB) // 128):
        st[pl.ds(n * 128, 128), :] = both[:, n * 128 : n * 128 + 128].T
    x = jnp.concatenate(
        [st[pl.ds(HIST - 2 * HH - back, ROWS, 2), :] for back in (0, 2)], 1
    )
    hi, lo = split(x)
    x = jnp.concatenate([hi, lo, hi], 1)
    eb = eb_ref[...]

    def keep(buf, i, value, layer, start):
        value = value * mask[layer, pl.ds(i, 1), :]
        value = jnp.concatenate([value[: HH - start] * m_time, value[HH - start :]], 0)
        hid[buf, i, start:ROWS] = value
        hi, lo = split(value)
        top[buf, i, start:ROWS] = hi
        low[buf, i, start:ROWS] = lo

    def encode(g, carry):
        y = jnp.dot(x, enc_ref[g], preferred_element_type=F32)
        for n in range(2):
            u = (y[:, n * 128 : n * 128 + 128] + eb) * 0.5
            keep(0, 2 * g + n, u + u * jnp.tanh(u), 0, 0)
        return carry

    lax.fori_loop(0, 8, encode, 0)
    low_half = lax.broadcasted_iota(jnp.int32, (1, 128), 1) < F
    for layer in range(LAYERS):
        d = 2**layer
        src, dst = layer % 2, 1 - layer % 2
        start = KEPT[layer + 1]
        begin = max(0, (start - d) // 16 * 16)
        bias = db_ref[layer : layer + 1, :]

        def dilated(i, carry, layer=layer, d=d, src=src, dst=dst, start=start, begin=begin, bias=bias):
            hi = [top[src, i + n, begin:ROWS] for n in range(2)]
            lo = [low[src, i + n, begin:ROWS] for n in range(2)]
            y = jnp.dot(jnp.concatenate(hi + lo + hi, 1), dil_ref[layer], preferred_element_type=F32)
            past = pltpu.roll(y[:, 128:], d, 0)[start - begin :]
            u = y[start - begin :, :128] + past + bias
            near, far = (i, i + 1) if src else (i + 1, i)
            h = jnp.where(low_half, hid[src, near, start:ROWS], hid[src, far, start:ROWS])
            keep(dst, i, h + u + u * jnp.tanh(u), layer + 1, start)
            return carry

        lax.fori_loop(0, PAIRS - 1 - layer, dilated, 0)
    start = KEPT[LAYERS]
    hi = jnp.concatenate([top[0, q, start:ROWS] for q in range(9)], 1)
    lo = jnp.concatenate([low[0, q, start:ROWS] for q in range(9)], 1)
    r = jnp.dot(hi, dec_ref[0], preferred_element_type=F32)
    r = r + jnp.dot(lo, dec_ref[0], preferred_element_type=F32)
    r = r + jnp.dot(hi, dec_ref[1], preferred_element_type=F32)
    past = pltpu.roll(r[:, 128:], 1, 0)[HH - start :]
    now = r[HH - start :, :128]
    wide[pl.ds(0, HB, 2), :] = now + past
    wide[pl.ds(1, HB, 2), :] = pltpu.roll(now, 96, 1)
    sums = []
    for n in range(2 * HB // TILE_T):
        cols = slice(n * TILE_T, n * TILE_T + TILE_T)
        out = wide[cols, :].T[: 2 * CB]
        recon_ref[:, cols] = out
        sq = (out - sig_ref[:, cols]) ** 2
        per = [jnp.sum(sq[m * TILE_C : m * TILE_C + TILE_C], keepdims=True) for m in range(2 * CB // TILE_C)]
        sums.append(jnp.concatenate(per, 0))
    err_ref[...] = jnp.concatenate(sums, 1) * (1.0 / (TILE_C * TILE_T))


def on_device(signal, encode_weight, encode_bias, dilated_weight, dilated_bias, decode_weight):
    vmem = pl.BlockSpec(memory_space=pltpu.VMEM)
    enc, dil, dec = pl.pallas_call(
        prepare,
        out_shape=(
            jax.ShapeDtypeStruct((8, 768, 256), BF),
            jax.ShapeDtypeStruct((LAYERS, 768, 256), BF),
            jax.ShapeDtypeStruct((2, 1152, 256), BF),
        ),
        in_specs=[vmem] * 3,
        out_specs=(vmem,) * 3,
        scratch_shapes=[pltpu.VMEM((256, 256), F32)],
        cost_estimate=pl.CostEstimate(flops=10**9, bytes_accessed=8 * 10**6, transcendentals=0),
        compiler_params=pltpu.CompilerParams(vmem_limit_bytes=32 * 2**20),
        name="prepare",
    )(encode_weight, dilated_weight, decode_weight)
    history = from_behind(signal[:, 2 * HB - HIST :], "tm", 1)
    whole = jnp.concatenate([history, signal], 1)
    below = from_behind(whole[2 * CB - EDGE :], "fiber", 1)
    above = from_behind(whole[:EDGE], "fiber", -1)
    eb = jnp.tile(encode_bias.reshape(1, F), (1, 2))
    db = jnp.tile(dilated_bias, (1, 2)) * 0.5
    return pl.pallas_call(
        score,
        out_shape=(
            jax.ShapeDtypeStruct((2 * CB, 2 * HB), F32),
            jax.ShapeDtypeStruct((2 * CB // TILE_C, 2 * HB // TILE_T), F32),
        ),
        in_specs=[vmem] * 9,
        out_specs=(vmem,) * 2,
        scratch_shapes=[
            pltpu.VMEM((HIST + 2 * HB, 128), F32),
            pltpu.VMEM((2, 16, ROWS, 128), F32),
            pltpu.VMEM((2, 16, ROWS, 128), BF),
            pltpu.VMEM((2, 16, ROWS, 128), BF),
            pltpu.VMEM((LAYERS + 1, 16, 128), F32),
            pltpu.VMEM((2 * HB, 128), F32),
        ],
        cost_estimate=pl.CostEstimate(flops=10**10, bytes_accessed=8 * 10**6, transcendentals=0),
        compiler_params=pltpu.CompilerParams(vmem_limit_bytes=48 * 2**20),
        name="score",
    )(signal, history, below, above, eb, db, enc, dil, dec)


def solution(mesh):
    return jax.shard_map(
        on_device,
        mesh=mesh,
        in_specs=(P("fiber", "tm"), P(), P(), P(), P(), P()),
        out_specs=(P("fiber", "tm"), P("fiber", "tm")),
        check_vma=False,
    )
```

profile of v0, /device:TPU:17, one launch (start us, length us, event | category | flops | bytes accessed | tf_op | source)
XLA Modules:
  0.0 47.9 jit_solution(8849842726698081534)
XLA Ops:
  0.6 0.0 copy-start
  0.6 0.8 %slice.9 = f32[32,256]{1,0:T(8,128)S(1)} slice(f32[32,512]{1,0:T(8,128)} %sig_ref.1), slice={[0:32], [256:512]} | slice | bytes 65536 | tf_op jit(solution)/shard_map/slice | solution.py:190
  1.5 3.1 %collective-permute-start = (f32[32,256]{1,0:T(8,128)S(1)}, f32[32,256]{1,0:T(8,128)S(1)}, u32[]{:S(2)}, u32[]{:S(2)}) collective-permute-start(f32[32,256]{1,0:T(8,128)S(1)} %slice.9), channel_id=1, source_target_pairs={{0,4},{4,8},{8,12},{12,16},{16,20},{20,24},{24,28},{1,5},{5,9},{9,... | collective-permute-start | bytes 98312 | tf_op jit(solution)/shard_map/ppermute | solution.py:32
  4.6 0.7 %broadcast_multiply_fusion = f32[6,64]{1,0:T(8,128)S(1)} fusion(f32[6,64]{1,0:T(8,128)} %param.10), kind=kLoop, calls=%fused_computation.2 | loop fusion | flops 384 | bytes 3072 | tf_op jit(solution)/shard_map/mul | solution.py:195
  5.3 0.7 %tile.6 = f32[2,64]{1,0:T(2,128)S(1)} broadcast(f32[64]{0:T(128)} %param.8), dimensions={1} | broadcast | bytes 768 | tf_op jit(solution)/shard_map/tile | solution.py:194
  5.9 0.1 tile.7.eb_ref
  6.0 0.1 mul.10.db_ref
  6.1 0.8 %copy.8.ew_ref = f32[64,9]{1,0:T(8,128)S(1)} copy(f32[64,9]{0,1:T(8,128)} %param.7) | data formatting | bytes 4608 | tf_op args[1]
  6.9 0.1 collective-permute-done.hist_ref
  7.0 0.8 %constant_dynamic-update-slice_fusion = f32[32,768]{1,0:T(8,128)S(1)} fusion(f32[32,768]{1,0:T(8,128)S(1)} %constant_dynamic-update-slice_fusion.1, f32[32,512]{1,0:T(8,128)} %sig_ref.1), kind=kLoop, calls=%fused_computation | loop fusion | bytes 131072 | tf_op jit(solution)/shard_map/concatenate | solution.py:191
  7.9 3.7 %collective-permute-start.2 = (f32[16,768]{1,0:T(8,128)S(1)}, f32[16,768]{1,0:T(8,128)S(1)}, u32[]{:S(2)}, u32[]{:S(2)}) collective-permute-start(f32[16,768]{1,0:T(8,128)S(1)} %get-tuple-element.8), channel_id=1, source_target_pairs={{1,0},{2,1},{3,2},{5,4},{6,5},{7,6},{9,8},{10,9},{11,10},{13,12},{... | collective-permute-start | bytes 147464 | tf_op jit(solution)/shard_map/ppermute | solution.py:32
  11.6 3.0 %collective-permute-start.1 = (f32[16,768]{1,0:T(8,128)S(1)}, f32[16,768]{1,0:T(8,128)S(1)}, u32[]{:S(2)}, u32[]{:S(2)}) collective-permute-start(f32[16,768]{1,0:T(8,128)S(1)} %get-tuple-element.9), channel_id=1, source_target_pairs={{0,1},{1,2},{2,3},{4,5},{5,6},{6,7},{8,9},{9,10},{10,11},{12,13},{... | collective-permute-start | bytes 147464 | tf_op jit(solution)/shard_map/ppermute | solution.py:32
  14.7 0.0 copy-start.1
  14.7 1.3 %copy-done.1 = f32[6,6,64,64]{3,2,1,0:T(8,128)S(1)} copy-done((f32[6,6,64,64]{3,2,1,0:T(8,128)S(1)}, f32[6,6,64,64]{3,2,1,0:T(8,128)}, u32[]{:S(2)}) %copy-start.1) | copy-done | bytes 589848
  15.9 0.0 copy-start.2
  15.9 0.7 %copy-done.2 = f32[9,64]{1,0:T(8,128)S(1)} copy-done((f32[9,64]{1,0:T(8,128)S(1)}, f32[9,64]{1,0:T(8,128)}, u32[]{:S(2)}) %copy-start.2) | copy-done | bytes 2328
  16.6 1.5 %prepare.1 = (bf16[8,768,256]{2,1,0:T(8,128)(2,1)S(1)}, bf16[6,768,256]{2,1,0:T(8,128)(2,1)S(1)}, bf16[2,1152,256]{2,1,0:T(8,128)(2,1)S(1)}) custom-call(f32[64,9]{1,0:T(8,128)S(1)} %copy.8.ew_ref, f32[6,6,64,64]{3,2,1,0:T(8,128)S(1)} %copy-done.1, f32[9,64]{1,0:T(8,128)S(1)} %copy-done.2), custom_call_target="tpu_custom_call" | custom-call | flops 1000000000 | bytes 8000000 | tf_op jit(solution)/shard_map/prepare/pallas_call | solution.py:176
  18.1 0.0 copy-start.3
  18.1 1.6 %copy-done.3 = bf16[8,768,256]{2,1,0:T(8,128)(2,1)} copy-done((bf16[8,768,256]{2,1,0:T(8,128)(2,1)}, bf16[8,768,256]{2,1,0:T(8,128)(2,1)S(1)}, u32[]{:S(2)}) %copy-start.3) | copy-done | bytes 3145752
  19.7 0.0 collective-permute-done.2.high_ref
  19.7 0.0 collective-permute-done.1.low_ref
  19.8 0.0 copy-done
  19.8 28.2 %score.1 = (f32[32,512]{1,0:T(8,128)}, f32[2,4]{1,0:T(2,128)}) custom-call(f32[32,512]{1,0:T(8,128)S(1)} %copy-done, f32[32,256]{1,0:T(8,128)S(1)} %collective-permute-done.hist_ref, f32[16,768]{1,0:T(8,128)S(1)} %collective-permute-done.1.low_ref, f32[16,768]{1,0:T(8,128)S(1)} %collective-permute-done.2.high_ref, f32[1,128]{1,0:T(1,128)S(1)} %tile.7.eb_ref, ...), custom_call_target="tpu_custom_call" | custom-call | flops 10000000000 | bytes 8000000 | tf_op jit(solution)/shard_map/score/pallas_call | solution.py:196
  (3 shorter events, 0.0 us)
Async XLA Ops:
  0.6 19.1 %copy-start = (f32[32,512]{1,0:T(8,128)S(1)}, f32[32,512]{1,0:T(8,128)}, u32[]{:S(2)}) copy-start(f32[32,512]{1,0:T(8,128)} %sig_ref.1) | copy-start | bytes 196612
  1.5 5.5 %collective-permute-start = (f32[32,256]{1,0:T(8,128)S(1)}, f32[32,256]{1,0:T(8,128)S(1)}, u32[]{:S(2)}, u32[]{:S(2)}) collective-permute-start(f32[32,256]{1,0:T(8,128)S(1)} %slice.9), channel_id=1, source_target_pairs={{0,4},{4,8},{8,12},{12,16},{16,20},{20,24},{24,28},{1,5},{5,9},{9,... | collective-permute-start | bytes 98312 | tf_op jit(solution)/shard_map/ppermute | solution.py:32
  7.9 11.9 %collective-permute-start.2 = (f32[16,768]{1,0:T(8,128)S(1)}, f32[16,768]{1,0:T(8,128)S(1)}, u32[]{:S(2)}, u32[]{:S(2)}) collective-permute-start(f32[16,768]{1,0:T(8,128)S(1)} %get-tuple-element.8), channel_id=1, source_target_pairs={{1,0},{2,1},{3,2},{5,4},{6,5},{7,6},{9,8},{10,9},{11,10},{13,12},{... | collective-permute-start | bytes 147464 | tf_op jit(solution)/shard_map/ppermute | solution.py:32
  11.6 8.1 %collective-permute-start.1 = (f32[16,768]{1,0:T(8,128)S(1)}, f32[16,768]{1,0:T(8,128)S(1)}, u32[]{:S(2)}, u32[]{:S(2)}) collective-permute-start(f32[16,768]{1,0:T(8,128)S(1)} %get-tuple-element.9), channel_id=1, source_target_pairs={{0,1},{1,2},{2,3},{4,5},{5,6},{6,7},{8,9},{9,10},{10,11},{12,13},{... | collective-permute-start | bytes 147464 | tf_op jit(solution)/shard_map/ppermute | solution.py:32
  14.7 1.3 %copy-start.1 = (f32[6,6,64,64]{3,2,1,0:T(8,128)S(1)}, f32[6,6,64,64]{3,2,1,0:T(8,128)}, u32[]{:S(2)}) copy-start(f32[6,6,64,64]{3,2,1,0:T(8,128)} %dw_ref.1) | copy-start | bytes 1769476
  15.9 0.7 %copy-start.2 = (f32[9,64]{1,0:T(8,128)S(1)}, f32[9,64]{1,0:T(8,128)}, u32[]{:S(2)}) copy-start(f32[9,64]{1,0:T(8,128)} %de_ref.1) | copy-start | bytes 6916
  18.1 1.6 %copy-start.3 = (bf16[8,768,256]{2,1,0:T(8,128)(2,1)}, bf16[8,768,256]{2,1,0:T(8,128)(2,1)S(1)}, u32[]{:S(2)}) copy-start(bf16[8,768,256]{2,1,0:T(8,128)(2,1)S(1)} %get-tuple-element.5.enc_ref) | copy-start | bytes 9437188
where the time goes:
time: 48.4 us; the launch traced here: 47.9 us
  Pallas kernels  29.6 us (61%)
  starting transfers between devices  9.89 us (20%)
  local copies, waits for them, and re-layouts  6.89 us (14%)
  between operations  0.7 us (1%)
  other arithmetic  0.69 us (1%)
    pallas_call x1, Pallas kernels, on_device(): pl.pallas_call(score, out_shape=(jax.ShapeDtypeStruct((2 * CB, 2 * HB), F...  28.2 us
    ppermute x3, starting transfers between devices, from_behind(): return lax.ppermute(block, axis, route)  9.89 us
    unnamed x10, local copies, waits for them, and re-layouts  4.39 us
    pallas_call x1, Pallas kernels, on_device(): pl.pallas_call(prepare, out_shape=(jax.ShapeDtypeStruct((8, 768, 256), BF...  1.46 us
  transfers between devices with their start and end apart: 3, of which 1 were waited for; matrix products, arithmetic and copies ran while one was open for 5% of the time, Pallas kernels for 3%

commit v1 on v0

--- a/solution.py
+++ b/solution.py
@@ -15,6 +15,7 @@
 ROWS = HH + HB
 PAIRS = (CB + 2 * LAYERS + 2) // 2
 KEPT = (0, 0, 0, 0, 0, 16, 48)
+GROUP = 3
 HIST = 256
 EDGE = 16
 BF = jnp.bfloat16
@@ -56,9 +57,8 @@
             parts += [r for r in rows if r.shape[0]]
         parts.append(none)
         hi, lo = split(jnp.concatenate(parts, 0))
-        enc_ref[g, 0:256] = hi
-        enc_ref[g, 256:512] = hi
-        enc_ref[g, 512:768] = lo
+        enc_ref[g, 0] = hi
+        enc_ref[g, 1] = lo
     zero = jnp.zeros((F, F), F32)
     for layer in range(LAYERS):
         odd = layer % 2
@@ -72,9 +72,9 @@
                 ]
                 wide[pl.ds((2 * lag + n) * F, F), :] = jnp.concatenate(cols, 1)
         hi, lo = split(wide[...].T)
-        dil_ref[layer, 0:256] = hi
-        dil_ref[layer, 256:512] = hi
-        dil_ref[layer, 512:768] = lo
+        dil_ref[layer, 0] = hi
+        dil_ref[layer, 1] = lo
+    dec_ref[4, :, 128:] = jnp.zeros((2, 128, 256), BF)
     for q in range(9):
         wide[...] = jnp.zeros((256, 256), F32)
         for s in range(2):
@@ -85,12 +85,13 @@
                     for b, at in enumerate((0, 32, 128)):
                         wide[at + p : at + p + 1, s * F : s * F + F] = de_ref[3 * a + b : 3 * a + b + 1, :]
         hi, lo = split(wide[:, 0:128].T)
-        dec_ref[0, q * 128 : q * 128 + 128] = hi
-        dec_ref[1, q * 128 : q * 128 + 128] = lo
+        at = q % 2 * 128
+        dec_ref[q // 2, 0, at : at + 128] = hi
+        dec_ref[q // 2, 1, at : at + 128] = lo
 
 
 def score(sig_ref, hist_ref, low_ref, high_ref, eb_ref, db_ref, enc_ref, dil_ref, dec_ref,
-          recon_ref, err_ref, st, hid, top, low, mask, wide):
+          recon_ref, err_ref, st, parts, hid, top, low, mask, wide, wide2):
     first = lax.axis_index("fiber") == 0
     last = lax.axis_index("fiber") == lax.axis_size("fiber") - 1
     m_low = jnp.where(first, 0.0, 1.0).astype(F32)
@@ -110,52 +111,117 @@
     x = jnp.concatenate(
         [st[pl.ds(HIST - 2 * HH - back, ROWS, 2), :] for back in (0, 2)], 1
     )
-    hi, lo = split(x)
-    x = jnp.concatenate([hi, lo, hi], 1)
+    parts[0], parts[1] = split(x)
     eb = eb_ref[...]
+    low_half = lax.broadcasted_iota(jnp.int32, (1, 128), 1) < F
 
     def keep(buf, i, value, layer, start):
-        value = value * mask[layer, pl.ds(i, 1), :]
+        value = value * mask[layer, i : i + 1, :]
         value = jnp.concatenate([value[: HH - start] * m_time, value[HH - start :]], 0)
         hid[buf, i, start:ROWS] = value
         hi, lo = split(value)
         top[buf, i, start:ROWS] = hi
         low[buf, i, start:ROWS] = lo
 
-    def encode(g, carry):
-        y = jnp.dot(x, enc_ref[g], preferred_element_type=F32)
+    def multiply(acc, lhs, weights):
         for n in range(2):
-            u = (y[:, n * 128 : n * 128 + 128] + eb) * 0.5
-            keep(0, 2 * g + n, u + u * jnp.tanh(u), 0, 0)
-        return carry
-
-    lax.fori_loop(0, 8, encode, 0)
-    low_half = lax.broadcasted_iota(jnp.int32, (1, 128), 1) < F
-    for layer in range(LAYERS):
+            pltpu.matmul_push_rhs(weights[0], 0, n)
+            pltpu.matmul_push_rhs(weights[1], 1, n)
+        for part, kind, load in ((0, 0, 0), (1, 0, None), (0, 1, 1)):
+            for g, pieces in enumerate(lhs):
+                for n in range(2):
+                    pltpu.matmul_acc_lhs(acc[n][g], pieces[part][n](), load if g == 0 else None)
+
+    def take(acc, g, rows):
+        return jnp.concatenate([pltpu.matmul_pop(acc[n][g])[: rows[n]] for n in range(2)], 0)
+
+    half = ROWS // 2
+
+    def encode(g):
+        def mm(acc):
+            lhs = [[[lambda k=k, n=n: parts[k, n * half : n * half + half] for n in range(2)] for k in range(2)]]
+            multiply(acc, lhs, (enc_ref[g, 0], enc_ref[g, 1]))
+
+        def finish(acc):
+            y = take(acc, 0, (half, half))
+            for n in range(2):
+                if 2 * g + n < PAIRS:
+                    u = (y[:, n * 128 : n * 128 + 128] + eb) * 0.5
+                    keep(0, 2 * g + n, u + u * jnp.tanh(u), 0, 0)
+
+        return mm, finish
+
+    def dilated(layer, pairs):
         d = 2**layer
         src, dst = layer % 2, 1 - layer % 2
         start = KEPT[layer + 1]
         begin = max(0, (start - d) // 16 * 16)
-        bias = db_ref[layer : layer + 1, :]
-
-        def dilated(i, carry, layer=layer, d=d, src=src, dst=dst, start=start, begin=begin, bias=bias):
-            hi = [top[src, i + n, begin:ROWS] for n in range(2)]
-            lo = [low[src, i + n, begin:ROWS] for n in range(2)]
-            y = jnp.dot(jnp.concatenate(hi + lo + hi, 1), dil_ref[layer], preferred_element_type=F32)
-            past = pltpu.roll(y[:, 128:], d, 0)[start - begin :]
-            u = y[start - begin :, :128] + past + bias
-            near, far = (i, i + 1) if src else (i + 1, i)
-            h = jnp.where(low_half, hid[src, near, start:ROWS], hid[src, far, start:ROWS])
-            keep(dst, i, h + u + u * jnp.tanh(u), layer + 1, start)
-            return carry
-
-        lax.fori_loop(0, PAIRS - 1 - layer, dilated, 0)
+
+        def piece(ref, i, n):
+            lo, hi = ((begin, half), (half, ROWS))[n]
+            if begin and n == 0:
+                lo = 0
+            return jnp.concatenate([ref[src, i, lo:hi], ref[src, i + 1, lo:hi]], 1)
+
+        def mm(acc):
+            lhs = [[[lambda ref=ref, i=i, n=n: piece(ref, i, n) for n in range(2)] for ref in (top, low)] for i in pairs]
+            multiply(acc, lhs, (dil_ref[layer, 0], dil_ref[layer, 1]))
+
+        def finish(acc):
+            bias = db_ref[layer : layer + 1, :]
+            for g, i in enumerate(pairs):
+                y = take(acc, g, (half, half))
+                past = pltpu.roll(y[:, 128:], d, 0)[start:]
+                u = y[start:, :128] + past + bias
+                near, far = (i, i + 1) if src else (i + 1, i)
+                h = jnp.where(low_half, hid[src, near, start:ROWS], hid[src, far, start:ROWS])
+                keep(dst, i, h + u + u * jnp.tanh(u), layer + 1, start)
+
+        return mm, finish
+
+    def decode():
+        edges = ((KEPT[LAYERS], 192), (192, ROWS))
+
+        def mm(acc):
+            def piece(ref, q, n):
+                lo, hi = edges[n]
+                two = [ref[0, i, lo:hi] for i in (q, min(q + 1, 8))]
+                return jnp.concatenate(two, 1)
+            for q in range(5):
+                for n in range(2):
+                    pltpu.matmul_push_rhs(dec_ref[q, 0], 0, n)
+                    pltpu.matmul_push_rhs(dec_ref[q, 1], 1, n)
+                for ref, load in ((top, 0), (low, None), (top, 1)):
+                    for n in range(2):
+                        pltpu.matmul_acc_lhs(acc[n], piece(ref, 2 * q, n), load)
+
+        return mm
+
+    tasks = [encode(g) for g in range(8)]
+    for layer in range(LAYERS):
+        count = PAIRS - 1 - layer
+        for i in range(0, count, GROUP):
+            tasks.append(dilated(layer, range(i, min(i + GROUP, count))))
+
+    def run(*refs):
+        sets = [[refs[(2 * s + n) * GROUP : (2 * s + n + 1) * GROUP] for n in range(2)] for s in range(2)]
+        tasks[0][0](sets[0])
+        for k, (_, finish) in enumerate(tasks):
+            if k + 1 < len(tasks):
+                tasks[k + 1][0](sets[(k + 1) % 2])
+            finish(sets[k % 2])
+
+    accs = [pltpu.ACC(n)((half, 256), F32) for s in range(2) for n in range(2) for g in range(GROUP)]
+    pl.run_scoped(run, *accs)
     start = KEPT[LAYERS]
-    hi = jnp.concatenate([top[0, q, start:ROWS] for q in range(9)], 1)
-    lo = jnp.concatenate([low[0, q, start:ROWS] for q in range(9)], 1)
-    r = jnp.dot(hi, dec_ref[0], preferred_element_type=F32)
-    r = r + jnp.dot(lo, dec_ref[0], preferred_element_type=F32)
-    r = r + jnp.dot(hi, dec_ref[1], preferred_element_type=F32)
+
+    def last(a0, a1):
+        decode()((a0, a1))
+        sums = jnp.concatenate([pltpu.matmul_pop(a0), pltpu.matmul_pop(a1)], 0)
+        wide2[...] = sums
+
+    pl.run_scoped(last, pltpu.ACC(0)((192 - start, 256), F32), pltpu.ACC(1)((ROWS - 192, 256), F32))
+    r = wide2[...]
     past = pltpu.roll(r[:, 128:], 1, 0)[HH - start :]
     now = r[HH - start :, :128]
     wide[pl.ds(0, HB, 2), :] = now + past
@@ -176,9 +242,9 @@
     enc, dil, dec = pl.pallas_call(
         prepare,
         out_shape=(
-            jax.ShapeDtypeStruct((8, 768, 256), BF),
-            jax.ShapeDtypeStruct((LAYERS, 768, 256), BF),
-            jax.ShapeDtypeStruct((2, 1152, 256), BF),
+            jax.ShapeDtypeStruct((8, 2, 256, 256), BF),
+            jax.ShapeDtypeStruct((LAYERS, 2, 256, 256), BF),
+            jax.ShapeDtypeStruct((5, 2, 256, 256), BF),
         ),
         in_specs=[vmem] * 3,
         out_specs=(vmem,) * 3,
@@ -203,11 +269,13 @@
         out_specs=(vmem,) * 2,
         scratch_shapes=[
             pltpu.VMEM((HIST + 2 * HB, 128), F32),
+            pltpu.VMEM((2, ROWS, 256), BF),
             pltpu.VMEM((2, 16, ROWS, 128), F32),
             pltpu.VMEM((2, 16, ROWS, 128), BF),
             pltpu.VMEM((2, 16, ROWS, 128), BF),
             pltpu.VMEM((LAYERS + 1, 16, 128), F32),
             pltpu.VMEM((2 * HB, 128), F32),
+            pltpu.VMEM((ROWS - KEPT[LAYERS], 256), F32),
         ],
         cost_estimate=pl.CostEstimate(flops=10**10, bytes_accessed=8 * 10**6, transcendentals=0),
         compiler_params=pltpu.CompilerParams(vmem_limit_bytes=48 * 2**20),

time: 48.4 us -> 31.1 us (0.64)
  the two profiles are of different devices: /device:TPU:17 before, /device:TPU:25 now
where the time goes in v1:
time: 31.1 us; the launch traced here: 30.7 us
  Pallas kernels  13.9 us (45%)
  starting transfers between devices  10 us (32%)
  local copies, waits for them, and re-layouts  5.19 us (17%)
  between operations  0.71 us (2%)
  other arithmetic  0.69 us (2%)
    pallas_call x1, Pallas kernels, on_device(): pl.pallas_call(score, out_shape=(jax.ShapeDtypeStruct((2 * CB, 2 * HB), F...  12.5 us
    ppermute x3, starting transfers between devices, from_behind(): return lax.ppermute(block, axis, route)  10 us
    unnamed x8, local copies, waits for them, and re-layouts  2.75 us
    pallas_call x1, Pallas kernels, on_device(): pl.pallas_call(prepare, out_shape=(jax.ShapeDtypeStruct((8, 2, 256, 256),...  1.41 us
    concatenate x1, local copies, waits for them, and re-layouts, on_device(): whole = jnp.concatenate([history, signal], 1)  0.84 us
    slice x1, local copies, waits for them, and re-layouts, on_device(): history = from_behind(signal[:, 2 * HB - HIST:], 'tm', 1)  0.76 us
    another operation x2, local copies, waits for them, and re-layouts, on_device(): eb = jnp.tile(encode_bias.reshape(1, F), (1, 2))  0.74 us
    mul x1, other arithmetic, on_device(): db = jnp.tile(dilated_bias, (1, 2)) * 0.5  0.69 us
  transfers between devices with their start and end apart: 3, of which 1 were waited for; matrix products, arithmetic and copies ran while one was open for 7% of the time, Pallas kernels for 5%

profile of v1, /device:TPU:25, one launch (start us, length us, event | category | flops | bytes accessed | tf_op | source)
XLA Modules:
  0.0 30.7 jit_solution(6774019628810692504)
XLA Ops:
  0.6 0.8 %slice.9 = f32[32,256]{1,0:T(8,128)S(1)} slice(f32[32,512]{1,0:T(8,128)} %sig_ref.1), slice={[0:32], [256:512]} | slice | bytes 65536 | tf_op jit(solution)/shard_map/slice | solution.py:256
  1.4 3.1 %collective-permute-start = (f32[32,256]{1,0:T(8,128)S(1)}, f32[32,256]{1,0:T(8,128)S(1)}, u32[]{:S(2)}, u32[]{:S(2)}) collective-permute-start(f32[32,256]{1,0:T(8,128)S(1)} %slice.9), channel_id=1, source_target_pairs={{0,4},{4,8},{8,12},{12,16},{16,20},{20,24},{24,28},{1,5},{5,9},{9,... | collective-permute-start | bytes 98312 | tf_op jit(solution)/shard_map/ppermute | solution.py:33
  4.5 0.7 %broadcast_multiply_fusion = f32[6,64]{1,0:T(8,128)S(1)} fusion(f32[6,64]{1,0:T(8,128)} %param.10), kind=kLoop, calls=%fused_computation.2 | loop fusion | flops 384 | bytes 3072 | tf_op jit(solution)/shard_map/mul | solution.py:261
  5.2 0.7 %tile.6 = f32[2,64]{1,0:T(2,128)S(1)} broadcast(f32[64]{0:T(128)} %param.8), dimensions={1} | broadcast | bytes 768 | tf_op jit(solution)/shard_map/tile | solution.py:260
  5.9 0.1 tile.7.eb_ref
  5.9 0.1 mul.10.db_ref
  6.0 0.8 %copy.8.ew_ref = f32[64,9]{1,0:T(8,128)S(1)} copy(f32[64,9]{0,1:T(8,128)} %param.7) | data formatting | bytes 4608 | tf_op args[1]
  6.8 0.1 collective-permute-done.hist_ref
  6.9 0.8 %constant_dynamic-update-slice_fusion = f32[32,768]{1,0:T(8,128)S(1)} fusion(f32[32,768]{1,0:T(8,128)S(1)} %constant_dynamic-update-slice_fusion.1, f32[32,512]{1,0:T(8,128)} %sig_ref.1), kind=kLoop, calls=%fused_computation | loop fusion | bytes 131072 | tf_op jit(solution)/shard_map/concatenate | solution.py:257
  7.8 3.7 %collective-permute-start.2 = (f32[16,768]{1,0:T(8,128)S(1)}, f32[16,768]{1,0:T(8,128)S(1)}, u32[]{:S(2)}, u32[]{:S(2)}) collective-permute-start(f32[16,768]{1,0:T(8,128)S(1)} %get-tuple-element.8), channel_id=1, source_target_pairs={{1,0},{2,1},{3,2},{5,4},{6,5},{7,6},{9,8},{10,9},{11,10},{13,12},{... | collective-permute-start | bytes 147464 | tf_op jit(solution)/shard_map/ppermute | solution.py:33
  11.5 0.0 copy-start
  11.6 3.2 %collective-permute-start.1 = (f32[16,768]{1,0:T(8,128)S(1)}, f32[16,768]{1,0:T(8,128)S(1)}, u32[]{:S(2)}, u32[]{:S(2)}) collective-permute-start(f32[16,768]{1,0:T(8,128)S(1)} %get-tuple-element.9), channel_id=1, source_target_pairs={{0,1},{1,2},{2,3},{4,5},{5,6},{6,7},{8,9},{9,10},{10,11},{12,13},{... | collective-permute-start | bytes 147464 | tf_op jit(solution)/shard_map/ppermute | solution.py:33
  14.7 0.0 copy-start.1
  14.7 1.3 %copy-done.1 = f32[6,6,64,64]{3,2,1,0:T(8,128)S(1)} copy-done((f32[6,6,64,64]{3,2,1,0:T(8,128)S(1)}, f32[6,6,64,64]{3,2,1,0:T(8,128)}, u32[]{:S(2)}) %copy-start.1) | copy-done | bytes 589848
  16.0 0.0 copy-start.2
  16.0 0.7 %copy-done.2 = f32[9,64]{1,0:T(8,128)S(1)} copy-done((f32[9,64]{1,0:T(8,128)S(1)}, f32[9,64]{1,0:T(8,128)}, u32[]{:S(2)}) %copy-start.2) | copy-done | bytes 2328
  16.7 1.4 %prepare.1 = (bf16[8,2,256,256]{3,2,1,0:T(8,128)(2,1)S(1)}, bf16[6,2,256,256]{3,2,1,0:T(8,128)(2,1)S(1)}, bf16[5,2,256,256]{3,2,1,0:T(8,128)(2,1)S(1)}) custom-call(f32[64,9]{1,0:T(8,128)S(1)} %copy.8.ew_ref, f32[6,6,64,64]{3,2,1,0:T(8,128)S(1)} %copy-done.1, f32[9,64]{1,0:T(8,128)S(1)} %copy-done.2), custom_call_target="tpu_custom_call" | custom-call | flops 1000000000 | bytes 8000000 | tf_op jit(solution)/shard_map/prepare/pallas_call | solution.py:242
  18.1 0.0 collective-permute-done.2.high_ref
  18.1 0.0 collective-permute-done.1.low_ref
  18.1 0.0 copy-done
  18.2 12.5 %score.1 = (f32[32,512]{1,0:T(8,128)}, f32[2,4]{1,0:T(2,128)}) custom-call(f32[32,512]{1,0:T(8,128)S(1)} %copy-done, f32[32,256]{1,0:T(8,128)S(1)} %collective-permute-done.hist_ref, f32[16,768]{1,0:T(8,128)S(1)} %collective-permute-done.1.low_ref, f32[16,768]{1,0:T(8,128)S(1)} %collective-permute-done.2.high_ref, f32[1,128]{1,0:T(1,128)S(1)} %tile.7.eb_ref, ...), custom_call_target="tpu_custom_call" | custom-call | flops 10000000000 | bytes 8000000 | tf_op jit(solution)/shard_map/score/pallas_call | solution.py:262
  (3 shorter events, 0.0 us)
Async XLA Ops:
  1.4 5.5 %collective-permute-start = (f32[32,256]{1,0:T(8,128)S(1)}, f32[32,256]{1,0:T(8,128)S(1)}, u32[]{:S(2)}, u32[]{:S(2)}) collective-permute-start(f32[32,256]{1,0:T(8,128)S(1)} %slice.9), channel_id=1, source_target_pairs={{0,4},{4,8},{8,12},{12,16},{16,20},{20,24},{24,28},{1,5},{5,9},{9,... | collective-permute-start | bytes 98312 | tf_op jit(solution)/shard_map/ppermute | solution.py:33
  7.8 10.3 %collective-permute-start.2 = (f32[16,768]{1,0:T(8,128)S(1)}, f32[16,768]{1,0:T(8,128)S(1)}, u32[]{:S(2)}, u32[]{:S(2)}) collective-permute-start(f32[16,768]{1,0:T(8,128)S(1)} %get-tuple-element.8), channel_id=1, source_target_pairs={{1,0},{2,1},{3,2},{5,4},{6,5},{7,6},{9,8},{10,9},{11,10},{13,12},{... | collective-permute-start | bytes 147464 | tf_op jit(solution)/shard_map/ppermute | solution.py:33
  11.5 6.6 %copy-start = (f32[32,512]{1,0:T(8,128)S(1)}, f32[32,512]{1,0:T(8,128)}, u32[]{:S(2)}) copy-start(f32[32,512]{1,0:T(8,128)} %sig_ref.1) | copy-start | bytes 196612
  11.6 6.6 %collective-permute-start.1 = (f32[16,768]{1,0:T(8,128)S(1)}, f32[16,768]{1,0:T(8,128)S(1)}, u32[]{:S(2)}, u32[]{:S(2)}) collective-permute-start(f32[16,768]{1,0:T(8,128)S(1)} %get-tuple-element.9), channel_id=1, source_target_pairs={{0,1},{1,2},{2,3},{4,5},{5,6},{6,7},{8,9},{9,10},{10,11},{12,13},{... | collective-permute-start | bytes 147464 | tf_op jit(solution)/shard_map/ppermute | solution.py:33
  14.7 1.3 %copy-start.1 = (f32[6,6,64,64]{3,2,1,0:T(8,128)S(1)}, f32[6,6,64,64]{3,2,1,0:T(8,128)}, u32[]{:S(2)}) copy-start(f32[6,6,64,64]{3,2,1,0:T(8,128)} %dw_ref.1) | copy-start | bytes 1769476
  16.0 0.7 %copy-start.2 = (f32[9,64]{1,0:T(8,128)S(1)}, f32[9,64]{1,0:T(8,128)}, u32[]{:S(2)}) copy-start(f32[9,64]{1,0:T(8,128)} %de_ref.1) | copy-start | bytes 6916

commit v2 on v1

--- a/solution.py
+++ b/solution.py
@@ -33,65 +33,65 @@
     return lax.ppermute(block, axis, route)
 
 
-def prepare(ew_ref, dw_ref, de_ref, enc_ref, dil_ref, dec_ref, wide):
-    ew = ew_ref[...]
-    k = lax.broadcasted_iota(jnp.int32, (9, 256), 0)
-    lane = lax.broadcasted_iota(jnp.int32, (9, 256), 1)
-    base = []
+def exchange(block, axis, first):
+    lows = range(first, lax.axis_size(axis) - 1, 2)
+    return lax.ppermute(block, axis, [p for i in lows for p in ((i, i + 1), (i + 1, i))])
+
+
+def encoder_weights(small_ref, enc_ref, wide):
+    ew = small_ref[0:9] * 0.5
+    wide[...] = jnp.zeros(wide.shape, F32)
     for j in range(4):
-        pick = (lane // F == k % 3) & (lane % F == 3 + 2 * j + k // 3)
-        base.append(
-            jnp.dot(ew, pick.astype(F32), precision=lax.Precision.HIGHEST,
-                    preferred_element_type=F32)
-        )
-    base = jnp.concatenate(base, 0).T
+        for a in range(3):
+            for b in range(3):
+                wide[b, 3 + 2 * j + a : 4 + 2 * j + a, j * F : j * F + F] = ew[3 * a + b : 3 * a + b + 1, :]
     none = jnp.zeros((F, 256), F32)
     for g in range(8):
         parts = []
         for b in range(3):
-            piece = base[b * F : b * F + 16]
+            piece = wide[b]
             if g < 7:
                 rows = [none[: 8 * g], piece, none[: F - 16 - 8 * g]]
             else:
                 rows = [none[: F - 8], piece[:8]]
             parts += [r for r in rows if r.shape[0]]
         parts.append(none)
-        hi, lo = split(jnp.concatenate(parts, 0))
-        enc_ref[g, 0] = hi
-        enc_ref[g, 1] = lo
+        enc_ref[g, 0], enc_ref[g, 1] = split(jnp.concatenate(parts, 0))
+
+
+def layer_weights(layer, dw_ref, dil_ref):
     zero = jnp.zeros((F, F), F32)
-    for layer in range(LAYERS):
-        odd = layer % 2
-        ins = (1, 0, 3, 2) if odd else (0, 1, 2, 3)
-        outs = (1, 2) if odd else (2, 1)
-        for lag in range(2):
-            for n, co in enumerate(outs):
-                cols = [
-                    dw_ref[layer, 2 * (ci - co + 1) + lag] * 0.5 if 0 <= ci - co + 1 <= 2 else zero
-                    for ci in ins
-                ]
-                wide[pl.ds((2 * lag + n) * F, F), :] = jnp.concatenate(cols, 1)
-        hi, lo = split(wide[...].T)
-        dil_ref[layer, 0] = hi
-        dil_ref[layer, 1] = lo
-    dec_ref[4, :, 128:] = jnp.zeros((2, 128, 256), BF)
-    for q in range(9):
-        wide[...] = jnp.zeros((256, 256), F32)
-        for s in range(2):
-            c = 2 * q + s
-            for a in range(3):
-                p = 2 * c + a - 1
-                if 0 <= p < 2 * CB:
-                    for b, at in enumerate((0, 32, 128)):
-                        wide[at + p : at + p + 1, s * F : s * F + F] = de_ref[3 * a + b : 3 * a + b + 1, :]
-        hi, lo = split(wide[:, 0:128].T)
-        at = q % 2 * 128
-        dec_ref[q // 2, 0, at : at + 128] = hi
-        dec_ref[q // 2, 1, at : at + 128] = lo
-
-
-def score(sig_ref, hist_ref, low_ref, high_ref, eb_ref, db_ref, enc_ref, dil_ref, dec_ref,
-          recon_ref, err_ref, st, parts, hid, top, low, mask, wide, wide2):
+    ins = (1, 0, 3, 2) if layer % 2 else (0, 1, 2, 3)
+    outs = (1, 2) if layer % 2 else (2, 1)
+    rows = []
+    for lag in range(2):
+        for co in outs:
+            cols = [
+                dw_ref[layer, 2 * (ci - co + 1) + lag] * 0.5 if 0 <= ci - co + 1 <= 2 else zero
+                for ci in ins
+            ]
+            rows.append(jnp.concatenate(cols, 1))
+    dil_ref[layer, 0], dil_ref[layer, 1] = split(jnp.concatenate(rows, 0).T)
+
+
+def decoder_weights(de, dec_ref, wide):
+    wide[...] = jnp.zeros(wide.shape, F32)
+    for c in range(CB + 1):
+        for a in range(3):
+            p = 2 * c + a - 1
+            if 0 <= p < 2 * CB:
+                for b, at in enumerate((0, 32, 128)):
+                    k = c % 4 * F
+                    wide[c // 4, at + p : at + p + 1, k : k + F] = de[3 * a + b : 3 * a + b + 1, :]
+    for q in range(5):
+        dec_ref[q, 0], dec_ref[q, 1] = split(wide[q].T)
+
+
+def score(sig_ref, hist_ref, near_ref, far_ref, small_ref, dw_ref, enc_ref,
+          recon_ref, err_ref, st, parts, hid, top, low, mask, wide, wide2, wide3, dil_ref, dec_ref):
+    small = small_ref[...]
+    bias = jnp.concatenate([small[18:25], small[18:25]], 1) * 0.5
+    layer_weights(0, dw_ref, dil_ref)
     first = lax.axis_index("fiber") == 0
     last = lax.axis_index("fiber") == lax.axis_size("fiber") - 1
     m_low = jnp.where(first, 0.0, 1.0).astype(F32)
@@ -103,8 +103,10 @@
         second = lane // F if layer % 2 == 0 else 1 - lane // F
         c = layer - LAYERS + 2 * pair + second
         mask[layer] = jnp.where(c < 0, m_low, jnp.where(c >= CB, m_high, 1.0))
-    own = jnp.concatenate([hist_ref[...], sig_ref[...]], 1)
-    s = jnp.concatenate([low_ref[...], own, high_ref[...]], 0)
+    own = jnp.concatenate([hist_ref[:, 2 * HB - HIST :], sig_ref[...]], 1)
+    even = lax.axis_index("fiber") % 2 == 0
+    near, far = near_ref[...], far_ref[...]
+    s = jnp.concatenate([jnp.where(even, far, near), own, jnp.where(even, near, far)], 0)
     both = jnp.concatenate([s, pltpu.roll(s, 1, 1)], 0)
     for n in range((HIST + 2 * HB) // 128):
         st[pl.ds(n * 128, 128), :] = both[:, n * 128 : n * 128 + 128].T
@@ -112,7 +114,7 @@
         [st[pl.ds(HIST - 2 * HH - back, ROWS, 2), :] for back in (0, 2)], 1
     )
     parts[0], parts[1] = split(x)
-    eb = eb_ref[...]
+    eb = bias[0:1]
     low_half = lax.broadcasted_iota(jnp.int32, (1, 128), 1) < F
 
     def keep(buf, i, value, layer, start):
@@ -146,7 +148,7 @@
             y = take(acc, 0, (half, half))
             for n in range(2):
                 if 2 * g + n < PAIRS:
-                    u = (y[:, n * 128 : n * 128 + 128] + eb) * 0.5
+                    u = y[:, n * 128 : n * 128 + 128] + eb
                     keep(0, 2 * g + n, u + u * jnp.tanh(u), 0, 0)
 
         return mm, finish
@@ -168,11 +170,11 @@
             multiply(acc, lhs, (dil_ref[layer, 0], dil_ref[layer, 1]))
 
         def finish(acc):
-            bias = db_ref[layer : layer + 1, :]
+            b = bias[layer + 1 : layer + 2]
             for g, i in enumerate(pairs):
                 y = take(acc, g, (half, half))
                 past = pltpu.roll(y[:, 128:], d, 0)[start:]
-                u = y[start:, :128] + past + bias
+                u = y[start:, :128] + past + b
                 near, far = (i, i + 1) if src else (i + 1, i)
                 h = jnp.where(low_half, hid[src, near, start:ROWS], hid[src, far, start:ROWS])
                 keep(dst, i, h + u + u * jnp.tanh(u), layer + 1, start)
@@ -197,16 +199,24 @@
 
         return mm
 
+    ahead = {}
     tasks = [encode(g) for g in range(8)]
     for layer in range(LAYERS):
         count = PAIRS - 1 - layer
         for i in range(0, count, GROUP):
             tasks.append(dilated(layer, range(i, min(i + GROUP, count))))
+            if i == 0:
+                if layer + 1 < LAYERS:
+                    ahead[len(tasks)] = lambda layer=layer: layer_weights(layer + 1, dw_ref, dil_ref)
+                else:
+                    ahead[len(tasks)] = lambda: decoder_weights(small[9:18], dec_ref, wide3)
 
     def run(*refs):
         sets = [[refs[(2 * s + n) * GROUP : (2 * s + n + 1) * GROUP] for n in range(2)] for s in range(2)]
         tasks[0][0](sets[0])
         for k, (_, finish) in enumerate(tasks):
+            if k in ahead:
+                ahead[k]()
             if k + 1 < len(tasks):
                 tasks[k + 1][0](sets[(k + 1) % 2])
             finish(sets[k % 2])
@@ -239,33 +249,33 @@
 
 def on_device(signal, encode_weight, encode_bias, dilated_weight, dilated_bias, decode_weight):
     vmem = pl.BlockSpec(memory_space=pltpu.VMEM)
-    enc, dil, dec = pl.pallas_call(
-        prepare,
-        out_shape=(
-            jax.ShapeDtypeStruct((8, 2, 256, 256), BF),
-            jax.ShapeDtypeStruct((LAYERS, 2, 256, 256), BF),
-            jax.ShapeDtypeStruct((5, 2, 256, 256), BF),
-        ),
-        in_specs=[vmem] * 3,
-        out_specs=(vmem,) * 3,
-        scratch_shapes=[pltpu.VMEM((256, 256), F32)],
-        cost_estimate=pl.CostEstimate(flops=10**9, bytes_accessed=8 * 10**6, transcendentals=0),
-        compiler_params=pltpu.CompilerParams(vmem_limit_bytes=32 * 2**20),
-        name="prepare",
-    )(encode_weight, dilated_weight, decode_weight)
-    history = from_behind(signal[:, 2 * HB - HIST :], "tm", 1)
-    whole = jnp.concatenate([history, signal], 1)
-    below = from_behind(whole[2 * CB - EDGE :], "fiber", 1)
-    above = from_behind(whole[:EDGE], "fiber", -1)
-    eb = jnp.tile(encode_bias.reshape(1, F), (1, 2))
-    db = jnp.tile(dilated_bias, (1, 2)) * 0.5
+    history = from_behind(signal, "tm", 1)
+    small = jnp.concatenate(
+        [encode_weight.T, decode_weight, encode_bias.reshape(1, F), dilated_bias], 0
+    )
+    enc = pl.pallas_call(
+        encoder_weights,
+        out_shape=jax.ShapeDtypeStruct((8, 2, 256, 256), BF),
+        in_specs=[vmem],
+        out_specs=vmem,
+        scratch_shapes=[pltpu.VMEM((3, 16, 256), F32)],
+        cost_estimate=pl.CostEstimate(flops=10**9, bytes_accessed=2 * 10**6, transcendentals=0),
+        compiler_params=pltpu.CompilerParams(vmem_limit_bytes=16 * 2**20),
+        name="encoder_weights",
+    )(small)
+    history, enc = lax.optimization_barrier((history, enc))
+    even = lax.axis_index("fiber") % 2 == 0
+    past = history[:, 2 * HB - HIST :]
+    bottom, top = (jnp.concatenate([past[rows], signal[rows]], 1) for rows in (slice(0, EDGE), slice(2 * CB - EDGE, 2 * CB)))
+    far = exchange(jnp.where(even, bottom, top), "fiber", 1)
+    near = exchange(jnp.where(even, top, bottom), "fiber", 0)
     return pl.pallas_call(
         score,
         out_shape=(
             jax.ShapeDtypeStruct((2 * CB, 2 * HB), F32),
             jax.ShapeDtypeStruct((2 * CB // TILE_C, 2 * HB // TILE_T), F32),
         ),
-        in_specs=[vmem] * 9,
+        in_specs=[vmem] * 7,
         out_specs=(vmem,) * 2,
         scratch_shapes=[
             pltpu.VMEM((HIST + 2 * HB, 128), F32),
@@ -276,11 +286,14 @@
             pltpu.VMEM((LAYERS + 1, 16, 128), F32),
             pltpu.VMEM((2 * HB, 128), F32),
             pltpu.VMEM((ROWS - KEPT[LAYERS], 256), F32),
+            pltpu.VMEM((5, 256, 256), F32),
+            pltpu.VMEM((LAYERS, 2, 256, 256), BF),
+            pltpu.VMEM((5, 2, 256, 256), BF),
         ],
         cost_estimate=pl.CostEstimate(flops=10**10, bytes_accessed=8 * 10**6, transcendentals=0),
         compiler_params=pltpu.CompilerParams(vmem_limit_bytes=48 * 2**20),
         name="score",
-    )(signal, history, below, above, eb, db, enc, dil, dec)
+    )(signal, history, near, far, small, dilated_weight, enc)
 
 
 def solution(mesh):

time: 31.1 us -> 26.3 us (0.85)
  the two profiles are of different devices: /device:TPU:25 before, /device:TPU:17 now
where the time goes in v2:
time: 26.3 us; the launch traced here: 26.1 us
  Pallas kernels  12.7 us (48%)
  starting transfers between devices  8.18 us (31%)
  waiting for transfers between devices  2.94 us (11%)
  local copies, waits for them, and re-layouts  0.82 us (3%)
  other arithmetic  0.77 us (3%)
  between operations  0.69 us (3%)
    pallas_call x1, Pallas kernels, on_device(): pl.pallas_call(score, out_shape=(jax.ShapeDtypeStruct((2 * CB, 2 * HB), F...  12.5 us
    ppermute x2, starting transfers between devices, exchange(): lax.ppermute(block, axis, [p for i in lows for p in ((i, i + 1), (i + 1,...  4.93 us
    ppermute x1, starting transfers between devices, from_behind(): return lax.ppermute(block, axis, route)  3.25 us
    ppermute x2, waiting for transfers between devices, exchange(): lax.ppermute(block, axis, [p for i in lows for p in ((i, i + 1), (i + 1,...  1.68 us
    ppermute x1, waiting for transfers between devices, from_behind(): return lax.ppermute(block, axis, route)  1.26 us
    slice x1, local copies, waits for them, and re-layouts, on_device(): signal[rows]  0.81 us
    concatenate x1, other arithmetic, on_device(): jnp.concatenate([encode_weight.T, decode_weight, encode_bias.reshape(1, F...  0.76 us
  transfers between devices with their start and end apart: 3, of which 2 were waited for; matrix products, arithmetic and copies ran while one was open for 6% of the time, Pallas kernels for 1%

profile of v2, /device:TPU:17, one launch (start us, length us, event | category | flops | bytes accessed | tf_op | source)
XLA Modules:
  0.0 26.1 jit_solution(4820485890781764191)
XLA Ops:
  0.6 0.0 copy-start
  0.6 0.0 copy-start.1
  0.6 3.3 %collective-permute-start = (f32[32,512]{1,0:T(8,128)}, f32[32,512]{1,0:T(8,128)S(1)}, u32[]{:S(2)}, u32[]{:S(2)}) collective-permute-start(f32[32,512]{1,0:T(8,128)} %sig_ref.1), channel_id=1, source_target_pairs={{0,4},{4,8},{8,12},{12,16},{16,20},{20,24},{24,28},{1,5},{5,9},{9,... | collective-permute-start | bytes 196616 | tf_op jit(solution)/shard_map/ppermute | solution.py:33
  3.9 0.8 %fusion.3 = (f32[16,512]{1,0:T(8,128)S(1)}, f32[16,512]{1,0:T(8,128)S(1)}) fusion(f32[32,512]{1,0:T(8,128)} %sig_ref.1), kind=kLoop, calls=%fused_computation.6 | loop fusion | bytes 131072 | tf_op jit(solution)/shard_map/slice | solution.py:269
  4.7 0.8 %pad_maximum_fusion.2.small_ref = f32[25,64]{1,0:T(8,128)S(1)} fusion(f32[6,64]{1,0:T(8,128)} %param.10, f32[1,64]{1,0:T(1,128)} %bitcast.3, f32[9,64]{1,0:T(8,128)} %param.11, f32[9,64]{1,0:T(8,128)} %bitcast.2), kind=kLoop, calls=%fused_computation.4 | loop fusion | flops 4800 | bytes 12800 | tf_op jit(solution)/shard_map/concatenate | solution.py:253
  5.5 0.2 encoder_weights.1.enc_ref
  5.6 1.3 %collective-permute-done.hist_ref = f32[32,512]{1,0:T(8,128)S(1)} collective-permute-done((f32[32,512]{1,0:T(8,128)}, f32[32,512]{1,0:T(8,128)S(1)}, u32[]{:S(2)}, u32[]{:S(2)}) %collective-permute-start) | collective-permute-done | bytes 65568 | tf_op jit(solution)/shard_map/ppermute | solution.py:33
  6.9 4.9 %collective-permute-start.2 = (f32[16,768]{1,0:T(8,128)S(1)}, f32[16,768]{1,0:T(8,128)S(1)}, u32[]{:S(2)}, u32[]{:S(2)}) collective-permute-start(f32[16,768]{1,0:T(8,128)S(1)} %get-tuple-element.6), channel_id=1, source_target_pairs={{1,2},{2,1},{5,6},{6,5},{9,10},{10,9},{13,14},{14,13},{17,18},{18,... | collective-permute-start | bytes 147464 | tf_op jit(solution)/shard_map/ppermute | solution.py:38
  11.8 0.1 collective-permute-start.1
  11.9 1.7 %collective-permute-done.2.far_ref = f32[16,768]{1,0:T(8,128)S(1)} collective-permute-done((f32[16,768]{1,0:T(8,128)S(1)}, f32[16,768]{1,0:T(8,128)S(1)}, u32[]{:S(2)}, u32[]{:S(2)}) %collective-permute-start.2) | collective-permute-done | bytes 49184 | tf_op jit(solution)/shard_map/ppermute | solution.py:38
  13.5 0.0 collective-permute-done.1.near_ref
  13.5 0.0 copy-done
  13.5 0.0 copy-done.1
  13.6 12.5 %score.1 = (f32[32,512]{1,0:T(8,128)}, f32[2,4]{1,0:T(2,128)}) custom-call(f32[32,512]{1,0:T(8,128)S(1)} %copy-done, f32[32,512]{1,0:T(8,128)S(1)} %collective-permute-done.hist_ref, f32[16,768]{1,0:T(8,128)S(1)} %collective-permute-done.1.near_ref, f32[16,768]{1,0:T(8,128)S(1)} %collective-permute-done.2.far_ref, f32[25,64]{1,0:T(8,128)S(1)} %pad_maximum_fusion.2.small_ref, ...), custom_call_target="tpu_custom_call" | custom-call | flops 10000000000 | bytes 8000000 | tf_op jit(solution)/shard_map/score/pallas_call | solution.py:272
  (2 shorter events, 0.0 us)
Async XLA Ops:
  0.6 12.9 %copy-start = (f32[32,512]{1,0:T(8,128)S(1)}, f32[32,512]{1,0:T(8,128)}, u32[]{:S(2)}) copy-start(f32[32,512]{1,0:T(8,128)} %sig_ref.1) | copy-start | bytes 196612
  0.6 12.9 %copy-start.1 = (f32[6,6,64,64]{3,2,1,0:T(8,128)S(1)}, f32[6,6,64,64]{3,2,1,0:T(8,128)}, u32[]{:S(2)}) copy-start(f32[6,6,64,64]{3,2,1,0:T(8,128)} %dw_ref.1) | copy-start | bytes 1769476
  0.6 6.3 %collective-permute-start = (f32[32,512]{1,0:T(8,128)}, f32[32,512]{1,0:T(8,128)S(1)}, u32[]{:S(2)}, u32[]{:S(2)}) collective-permute-start(f32[32,512]{1,0:T(8,128)} %sig_ref.1), channel_id=1, source_target_pairs={{0,4},{4,8},{8,12},{12,16},{16,20},{20,24},{24,28},{1,5},{5,9},{9,... | collective-permute-start | bytes 196616 | tf_op jit(solution)/shard_map/ppermute | solution.py:33
  6.9 6.6 %collective-permute-start.2 = (f32[16,768]{1,0:T(8,128)S(1)}, f32[16,768]{1,0:T(8,128)S(1)}, u32[]{:S(2)}, u32[]{:S(2)}) collective-permute-start(f32[16,768]{1,0:T(8,128)S(1)} %get-tuple-element.6), channel_id=1, source_target_pairs={{1,2},{2,1},{5,6},{6,5},{9,10},{10,9},{13,14},{14,13},{17,18},{18,... | collective-permute-start | bytes 147464 | tf_op jit(solution)/shard_map/ppermute | solution.py:38
  11.8 1.8 %collective-permute-start.1 = (f32[16,768]{1,0:T(8,128)S(1)}, f32[16,768]{1,0:T(8,128)S(1)}, u32[]{:S(2)}, u32[]{:S(2)}) collective-permute-start(f32[16,768]{1,0:T(8,128)S(1)} %get-tuple-element.7), channel_id=1, source_target_pairs={{0,1},{1,0},{2,3},{3,2},{4,5},{5,4},{6,7},{7,6},{8,9},{9,8},{10,11... | collective-permute-start | bytes 147464 | tf_op jit(solution)/shard_map/ppermute | solution.py:38

commit v3 on v2

v3 whole, which is shorter than its diff:
```python
import functools

import jax
import jax.numpy as jnp
from jax import lax
from jax.experimental import pallas as pl
from jax.experimental.pallas import tpu as pltpu
from jax.sharding import PartitionSpec as P

LAYERS = 6
F = 64
TILE_C = 16
TILE_T = 128
CB = 16
HB = 256
HH = 64
ROWS = HH + HB
PAIRS = (CB + 2 * LAYERS + 2) // 2
LATER = ((64, 320), (64, 320), (64, 320), (64, 320), (80, 320), (96, 320), (128, 320))
EARLIER = ((0, 80), (0, 80), (0, 80), (0, 80), (0, 80), (16, 96), (48, 128))
CHUNK = 16
SLOTS = 32
HIST = 256
EDGE = 16
BF = jnp.bfloat16
F32 = jnp.float32


def split(x):
    hi = x.astype(BF)
    return hi, (x - hi.astype(F32)).astype(BF)


def from_behind(block, axis, distance):
    devices = range(lax.axis_size(axis))
    route = [(i - distance, i) for i in devices if i - distance in devices]
    return lax.ppermute(block, axis, route)


def exchange(block, axis, first):
    lows = range(first, lax.axis_size(axis) - 1, 2)
    return lax.ppermute(block, axis, [p for i in lows for p in ((i, i + 1), (i + 1, i))])


def encoder_weights(small_ref, enc_ref, wide):
    ew = small_ref[0:9] * 0.5
    wide[...] = jnp.zeros(wide.shape, F32)
    for j in range(4):
        for a in range(3):
            for b in range(3):
                wide[b, 3 + 2 * j + a : 4 + 2 * j + a, j * F : j * F + F] = ew[3 * a + b : 3 * a + b + 1, :]
    none = jnp.zeros((F, 256), F32)
    for g in range(8):
        parts = []
        for b in range(3):
            piece = wide[b]
            if g < 7:
                rows = [none[: 8 * g], piece, none[: F - 16 - 8 * g]]
            else:
                rows = [none[: F - 8], piece[:8]]
            parts += [r for r in rows if r.shape[0]]
        parts.append(none)
        enc_ref[g, 0], enc_ref[g, 1] = split(jnp.concatenate(parts, 0))


def layer_weights(layer, dw_ref, dil_ref):
    zero = jnp.zeros((F, F), F32)
    ins = (1, 0, 3, 2) if layer % 2 else (0, 1, 2, 3)
    outs = (1, 2) if layer % 2 else (2, 1)
    rows = []
    for lag in range(2):
        for co in outs:
            cols = [
                dw_ref[layer, 2 * (ci - co + 1) + lag] * 0.5 if 0 <= ci - co + 1 <= 2 else zero
                for ci in ins
            ]
            rows.append(jnp.concatenate(cols, 1))
    dil_ref[layer, 0], dil_ref[layer, 1] = split(jnp.concatenate(rows, 0).T)


def decoder_weights(de, dec_ref, wide):
    wide[...] = jnp.zeros(wide.shape, F32)
    for c in range(CB + 1):
        for a in range(3):
            p = 2 * c + a - 1
            if 0 <= p < 2 * CB:
                for b in range(3):
                    k, at = c % 4 * F, b * 2 * CB + p
                    wide[c // 4, at : at + 1, k : k + F] = de[3 * a + b : 3 * a + b + 1, :]
    for q in range(5):
        hi, lo = split(wide[q].T)
        dec_ref[q] = jnp.concatenate([hi, lo], 1)


def edge_masks(mask):
    m_low = jnp.where(lax.axis_index("fiber") == 0, 0.0, 1.0).astype(F32)
    m_high = jnp.where(lax.axis_index("fiber") == lax.axis_size("fiber") - 1, 0.0, 1.0).astype(F32)
    pair = lax.broadcasted_iota(jnp.int32, (16, 128), 0)
    lane = lax.broadcasted_iota(jnp.int32, (16, 128), 1)
    for layer in range(LAYERS + 1):
        second = lane // F if layer % 2 == 0 else 1 - lane // F
        c = layer - LAYERS + 2 * pair + second
        mask[layer] = jnp.where(c < 0, m_low, jnp.where(c >= CB, m_high, 1.0))


def gather_taps(s, st, first, begin, count, parts, groups):
    both = jnp.concatenate([s, pltpu.roll(s, 1, 1)], 0)
    for n in range(s.shape[1] // 128):
        st[pl.ds(first + n * 128, 128), :] = both[:, n * 128 : n * 128 + 128].T
    x = [st[pl.ds(HIST + 2 * (begin - HH) - back, count, 2), :] for back in (0, 2)]
    for g in range(groups):
        rolled = [pltpu.roll(half, 128 - 8 * g, 1) if g else half for half in x]
        parts[g, 0, begin : begin + count], parts[g, 1, begin : begin + count] = split(jnp.concatenate(rolled, 1))


def network(ranges, parts, hid, top, low, mask, bias, enc_ref, dil_ref, dec_ref, encodes, group, ahead, kept, finished):
    eb = bias[0:1]
    low_half = lax.broadcasted_iota(jnp.int32, (1, 128), 1) < F
    m_time = jnp.where(lax.axis_index("tm") == 0, 0.0, 1.0).astype(F32)

    def keep(buf, i, value, layer):
        start, end = ranges[layer]
        value = value * mask[layer, i : i + 1, :]
        if start < HH:
            value = jnp.concatenate([value[: HH - start] * m_time, value[HH - start :]], 0)
        hid[buf, i, start:end] = value
        top[buf, i, start:end], low[buf, i, start:end] = split(value)
        kept(layer, i, value)

    def chunks(pairs, begin, end):
        units = [(i, r) for i in pairs for r in range(begin, end, CHUNK)]
        half = (len(units) + 1) // 2
        return units[:half], units[half:]

    def multiply(acc, units, piece, steps):
        for step, weights in enumerate(steps):
            for n in range(2):
                for k, matrix in enumerate(weights):
                    pltpu.matmul_push_rhs(matrix, k, n)
            for part, load in ((0, 0), (1, None), (0, 1))[: len(weights) + 1]:
                for n in range(2):
                    for slot, unit in enumerate(units[n]):
                        pltpu.matmul_acc_lhs(acc[n][slot], piece(part, step, unit), load if slot == 0 else None)

    def take(acc, units, i):
        out = [pltpu.matmul_pop(acc[n][slot]) for n in range(2) for slot, unit in enumerate(units[n]) if unit[0] == i]
        return jnp.concatenate(out, 0)

    def encode(groups):
        units = chunks(groups, *ranges[0])

        def mm(acc):
            g, same = (0, parts.shape[0] == 1) if len(groups) > 1 else (groups[0], True)
            multiply(acc, units, lambda part, step, unit: parts[0 if same else unit[0], part, unit[1] : unit[1] + CHUNK],
                     ((enc_ref[g, 0], enc_ref[g, 1]),))

        def finish(acc):
            for g in groups:
                y = take(acc, units, g)
                for n in range(2):
                    if 2 * g + n < PAIRS:
                        u = y[:, n * 128 : n * 128 + 128] + eb
                        keep(0, 2 * g + n, u + u * jnp.tanh(u), 0)

        return mm, finish

    def dilated(layer, pairs):
        d = 2**layer
        src, dst = layer % 2, 1 - layer % 2
        start, end = ranges[layer + 1]
        begin = max(ranges[layer][0], (start - d) // CHUNK * CHUNK)
        units = chunks(pairs, begin, end)

        def piece(part, step, unit):
            i, r = unit
            ref = low if part else top
            return jnp.concatenate([ref[src, i, r : r + CHUNK], ref[src, i + 1, r : r + CHUNK]], 1)

        def mm(acc):
            multiply(acc, units, piece, ((dil_ref[layer, 0], dil_ref[layer, 1]),))

        def finish(acc):
            for i in pairs:
                y = take(acc, units, i)
                past = pltpu.roll(y[:, 128:], d, 0)[start - begin :]
                u = y[start - begin :, :128] + past + bias[layer + 1 : layer + 2]
                near, far = (i, i + 1) if src else (i + 1, i)
                h = jnp.where(low_half, hid[src, near, start:end], hid[src, far, start:end])
                keep(dst, i, h + u + u * jnp.tanh(u), layer + 1)

        return mm, finish

    def decode():
        units = chunks((0,), *ranges[LAYERS])

        def piece(part, step, unit):
            ref, r = low if part else top, unit[1]
            return jnp.concatenate([ref[0, i, r : r + CHUNK] for i in (2 * step, min(2 * step + 1, 8))], 1)

        def mm(acc):
            multiply(acc, units, piece, [(dec_ref[q],) for q in range(5)])

        def finish(acc):
            y = take(acc, units, 0)
            finished(y[:, :128] + y[:, 128:])

        return mm, finish

    tasks = [encode(range(g, g + encodes)) for g in range(0, 8, encodes)]
    for layer in range(LAYERS):
        count = PAIRS - 1 - layer
        tasks += [dilated(layer, range(i, min(i + group, count))) for i in range(0, count, group)]
        tasks.append(lambda layer=layer: ahead(layer))
    tasks.append(decode())

    def run(*refs):
        sets = [[refs[(2 * s + n) * SLOTS : (2 * s + n + 1) * SLOTS] for n in range(2)] for s in range(2)]
        waiting, turn = None, 0
        for task in tasks:
            if callable(task):
                task()
                continue
            if task is tasks[-1] and waiting:
                waiting()
                waiting = None
            mm, finish = task
            mm(sets[turn])
            if waiting:
                waiting()
            waiting = functools.partial(finish, sets[turn])
            turn = 1 - turn
        waiting()

    pl.run_scoped(run, *[pltpu.ACC(n)((CHUNK, 256), F32) for s in range(2) for n in range(2) for k in range(SLOTS)])


def later(s_ref, small_ref, dw_ref, enc_ref, sums_ref, h4_ref, h5_ref, dil_ref, dec_ref, st, hid, top, low, mask, parts, wide):
    small = small_ref[...]
    bias = jnp.concatenate([small[18:25], small[18:25]], 1) * 0.5
    layer_weights(0, dw_ref, dil_ref)
    edge_masks(mask)
    st[HIST - 8 : HIST, :] = jnp.zeros((8, 128), F32)
    gather_taps(s_ref[...], st, HIST, HH, HB, parts, 1)

    def ahead(layer):
        if layer + 1 < LAYERS:
            layer_weights(layer + 1, dw_ref, dil_ref)
        if layer == 2:
            decoder_weights(small[9:18], dec_ref, wide)

    def kept(layer, i, value):
        if layer == 4:
            h4_ref[i] = value[:16]
        if layer == 5:
            h5_ref[i] = value[:32]

    def finished(sums):
        sums_ref[...] = sums

    network(LATER, parts, hid, top, low, mask, bias, enc_ref, dil_ref, dec_ref, 1, 3, ahead, kept, finished)


def earlier(s_ref, hist_ref, small_ref, enc_ref, sums_ref, h4_ref, h5_ref, dil_ref, dec_ref,
            recon_ref, err_ref, st, hid, top, low, mask, parts, wide, whole):
    small = small_ref[...]
    bias = jnp.concatenate([small[18:25], small[18:25]], 1) * 0.5
    edge_masks(mask)
    gather_taps(jnp.concatenate([hist_ref[...], s_ref[:, :128]], 1), st, 0, 0, EARLIER[0][1], parts, 8)
    for buf, ref, begin, end in ((0, h4_ref, 80, 96), (1, h5_ref, 96, 128)):
        for i in range(ref.shape[0]):
            value = ref[i]
            hid[buf, i, begin:end] = value
            top[buf, i, begin:end], low[buf, i, begin:end] = split(value)

    base = EARLIER[LAYERS][0]
    whole[EARLIER[LAYERS][1] - base :, :] = sums_ref[...]

    def scores(tiles):
        begin, count = HH - base + tiles[0] * TILE_T // 2, len(tiles) * TILE_T // 2
        now, past = whole[begin : begin + count, :], whole[begin - 1 : begin - 1 + count, :]
        wide[pl.ds(tiles[0] * TILE_T, count, 2), :] = now + pltpu.roll(past, 128 - 4 * CB, 1)
        wide[pl.ds(tiles[0] * TILE_T + 1, count, 2), :] = pltpu.roll(now, 128 - 2 * CB, 1)
        for n in tiles:
            cols = slice(n * TILE_T, n * TILE_T + TILE_T)
            out = wide[cols, :].T[: 2 * CB]
            recon_ref[:, cols] = out
            sq = (out - s_ref[EDGE : EDGE + 2 * CB, cols]) ** 2
            per = [jnp.sum(sq[m * TILE_C : m * TILE_C + TILE_C], keepdims=True) for m in range(2 * CB // TILE_C)]
            err_ref[:, n : n + 1] = jnp.concatenate(per, 0) * (1.0 / (TILE_C * TILE_T))

    def ahead(layer):
        if layer == 1:
            scores((2, 3))

    def finished(value):
        whole[: EARLIER[LAYERS][1] - base, :] = value

    network(EARLIER, parts, hid, top, low, mask, bias, enc_ref, dil_ref, dec_ref, 4, 4, ahead,
            lambda layer, i, value: None, finished)
    scores((0, 1))


def on_device(signal, encode_weight, encode_bias, dilated_weight, dilated_bias, decode_weight):
    vmem = pl.BlockSpec(memory_space=pltpu.VMEM)
    far = exchange(signal, "fiber", 1)
    small = jnp.concatenate(
        [encode_weight.T, decode_weight, encode_bias.reshape(1, F), dilated_bias], 0
    )
    own, small = lax.optimization_barrier((signal, small))
    near = exchange(own, "fiber", 0)
    enc = pl.pallas_call(
        encoder_weights,
        out_shape=jax.ShapeDtypeStruct((8, 2, 256, 256), BF),
        in_specs=[vmem],
        out_specs=vmem,
        scratch_shapes=[pltpu.VMEM((3, 16, 256), F32)],
        cost_estimate=pl.CostEstimate(flops=10**9, bytes_accessed=2 * 10**6, transcendentals=0),
        compiler_params=pltpu.CompilerParams(vmem_limit_bytes=16 * 2**20),
        name="encoder_weights",
    )(small)
    near, far, enc = lax.optimization_barrier((near, far, enc))
    even = lax.axis_index("fiber") % 2 == 0
    below = jnp.where(even, far[2 * CB - EDGE :], near[2 * CB - EDGE :])
    above = jnp.where(even, near[:EDGE], far[:EDGE])
    section = jnp.concatenate([below, signal, above], 0)
    history = from_behind(section[:, 2 * HB - HIST :], "tm", 1)
    scratch = [
        pltpu.VMEM((HIST + 2 * HB, 128), F32),
        pltpu.VMEM((2, 16, ROWS, 128), F32),
        pltpu.VMEM((2, 16, ROWS, 128), BF),
        pltpu.VMEM((2, 16, ROWS, 128), BF),
        pltpu.VMEM((LAYERS + 1, 16, 128), F32),
    ]
    params = pltpu.CompilerParams(vmem_limit_bytes=32 * 2**20)
    sums, h4, h5, dil, dec = pl.pallas_call(
        later,
        out_shape=(
            jax.ShapeDtypeStruct((LATER[LAYERS][1] - LATER[LAYERS][0], 128), F32),
            jax.ShapeDtypeStruct((PAIRS - 4, 16, 128), F32),
            jax.ShapeDtypeStruct((PAIRS - 5, 32, 128), F32),
            jax.ShapeDtypeStruct((LAYERS, 2, 256, 256), BF),
            jax.ShapeDtypeStruct((5, 256, 256), BF),
        ),
        in_specs=[vmem] * 4,
        out_specs=(vmem,) * 5,
        scratch_shapes=scratch + [pltpu.VMEM((1, 2, ROWS, 256), BF), pltpu.VMEM((5, 128, 256), F32)],
        cost_estimate=pl.CostEstimate(flops=8 * 10**9, bytes_accessed=8 * 10**6, transcendentals=0),
        compiler_params=params,
        name="later",
    )(section, small, dilated_weight, enc)
    return pl.pallas_call(
        earlier,
        out_shape=(
            jax.ShapeDtypeStruct((2 * CB, 2 * HB), F32),
            jax.ShapeDtypeStruct((2 * CB // TILE_C, 2 * HB // TILE_T), F32),
        ),
        in_specs=[vmem] * 9,
        out_specs=(vmem,) * 2,
        scratch_shapes=scratch
        + [pltpu.VMEM((8, 2, EARLIER[0][1], 256), BF), pltpu.VMEM((2 * HB, 128), F32), pltpu.VMEM((ROWS - EARLIER[LAYERS][0], 128), F32)],
        cost_estimate=pl.CostEstimate(flops=2 * 10**9, bytes_accessed=8 * 10**6, transcendentals=0),
        compiler_params=params,
        name="earlier",
    )(section, history, small, enc, sums, h4, h5, dil, dec)


def solution(mesh):
    return jax.shard_map(
        on_device,
        mesh=mesh,
        in_specs=(P("fiber", "tm"), P(), P(), P(), P(), P()),
        out_specs=(P("fiber", "tm"), P("fiber", "tm")),
        check_vma=False,
    )
```

time: 26.3 us -> 24.6 us (0.935)
  the two profiles are of different devices: /device:TPU:17 before, /device:TPU:0 now
where the time goes in v3:
time: 24.6 us; the launch traced here: 24.3 us
  Pallas kernels  13.4 us (54%)
  starting transfers between devices  8.46 us (34%)
  waiting for transfers between devices  0.96 us (4%)
  other arithmetic  0.78 us (3%)
  between operations  0.71 us (3%)
    pallas_call x1, Pallas kernels, on_device(): pl.pallas_call(later, out_shape=(jax.ShapeDtypeStruct((LATER[LAYERS][1] -...  8.93 us
    ppermute x2, starting transfers between devices, exchange(): lax.ppermute(block, axis, [p for i in lows for p in ((i, i + 1), (i + 1,...  5.06 us
    pallas_call x1, Pallas kernels, on_device(): pl.pallas_call(earlier, out_shape=(jax.ShapeDtypeStruct((2 * CB, 2 * HB),...  4.35 us
    ppermute x1, starting transfers between devices, from_behind(): return lax.ppermute(block, axis, route)  3.4 us
    ppermute x2, waiting for transfers between devices, exchange(): lax.ppermute(block, axis, [p for i in lows for p in ((i, i + 1), (i + 1,...  0.95 us
    concatenate x1, other arithmetic, on_device(): jnp.concatenate([encode_weight.T, decode_weight, encode_bias.reshape(1, F...  0.76 us
  transfers between devices with their start and end apart: 3, of which 1 were waited for; matrix products, arithmetic and copies ran while one was open for 3% of the time, Pallas kernels for 37%

profile of v3, /device:TPU:0, one launch (start us, length us, event | category | flops | bytes accessed | tf_op | source)
XLA Modules:
  0.0 24.3 jit_solution(6542065437729305538)
XLA Ops:
  0.6 0.7 %collective-permute-start.1 = (f32[32,512]{1,0:T(8,128)}, f32[32,512]{1,0:T(8,128)S(1)}, u32[]{:S(2)}, u32[]{:S(2)}) collective-permute-start(f32[32,512]{1,0:T(8,128)} %param.6), channel_id=1, source_target_pairs={{1,2},{2,1},{5,6},{6,5},{9,10},{10,9},{13,14},{14,13},{17,18},{18,... | collective-permute-start | bytes 196616 | tf_op jit(solution)/shard_map/ppermute | solution.py:42
  1.3 0.8 %pad_maximum_fusion.1.small_ref = f32[25,64]{1,0:T(8,128)S(1)} fusion(f32[6,64]{1,0:T(8,128)} %param.10, f32[1,64]{1,0:T(1,128)} %bitcast.3, f32[9,64]{1,0:T(8,128)} %param.11, f32[9,64]{1,0:T(8,128)} %bitcast.2), kind=kLoop, calls=%fused_computation.3 | loop fusion | flops 4800 | bytes 12800 | tf_op jit(solution)/shard_map/concatenate | solution.py:306
  2.1 4.4 %collective-permute-start = (f32[32,512]{1,0:T(8,128)}, f32[32,512]{1,0:T(8,128)S(1)}, u32[]{:S(2)}, u32[]{:S(2)}) collective-permute-start(f32[32,512]{1,0:T(8,128)} %param.6), channel_id=1, source_target_pairs={{0,1},{1,0},{2,3},{3,2},{4,5},{5,4},{6,7},{7,6},{8,9},{9,8},{10,11... | collective-permute-start | bytes 196616 | tf_op jit(solution)/shard_map/ppermute | solution.py:42
  6.5 0.0 copy-start.1
  6.5 0.0 copy-start
  6.5 0.2 encoder_weights.1.enc_ref
  6.6 1.0 %collective-permute-done = f32[32,512]{1,0:T(8,128)S(1)} collective-permute-done((f32[32,512]{1,0:T(8,128)}, f32[32,512]{1,0:T(8,128)S(1)}, u32[]{:S(2)}, u32[]{:S(2)}) %collective-permute-start) | collective-permute-done | bytes 65568 | tf_op jit(solution)/shard_map/ppermute | solution.py:42
  7.6 0.0 collective-permute-done.1
  7.6 0.0 copy-done.1
  7.6 3.4 %collective-permute-start.2 = (f32[64,256]{1,0:T(8,128)S(1)}, f32[64,256]{1,0:T(8,128)S(1)}, u32[]{:S(2)}, u32[]{:S(2)}) collective-permute-start(f32[64,256]{1,0:T(8,128)S(1)} %slice.20), channel_id=1, source_target_pairs={{0,4},{4,8},{8,12},{12,16},{16,20},{20,24},{24,28},{1,5},{5,9},{9,... | collective-permute-start | bytes 196616 | tf_op jit(solution)/shard_map/ppermute | solution.py:37
  11.0 0.0 copy-done
  11.0 8.9 %later.1 = (f32[192,128]{1,0:T(8,128)S(1)}, f32[11,16,128]{2,1,0:T(8,128)S(1)}, f32[10,32,128]{2,1,0:T(8,128)S(1)}, bf16[6,2,256,256]{3,2,1,0:T(8,128)(2,1)S(1)}, bf16[5,256,256]{2,1,0:T(8,128)(2,1)S(1)}) custom-call(f32[64,512]{1,0:T(8,128)S(1)} %pad_maximum_fusion.s_ref, f32[25,64]{1,0:T(8,128)S(1)} %pad_maximum_fusion.1.small_ref, ...), custom_call_target="tpu_custom_call" | custom-call | flops 8000000000 | bytes 8000000 | tf_op jit(solution)/shard_map/later/pallas_call | solution.py:335
  20.0 0.0 collective-permute-done.2.hist_ref
  20.0 4.3 %earlier.1 = (f32[32,512]{1,0:T(8,128)}, f32[2,4]{1,0:T(2,128)}) custom-call(f32[64,512]{1,0:T(8,128)S(1)} %pad_maximum_fusion.s_ref, f32[64,256]{1,0:T(8,128)S(1)} %collective-permute-done.2.hist_ref, f32[25,64]{1,0:T(8,128)S(1)} %pad_maximum_fusion.1.small_ref, bf16[8,2,256,256]{3,2,1,0:T(8,128)(2,1)S(1)} %encoder_weights.1.enc_ref, ...), custom_call_target="tpu_custom_call" | custom-call | flops 2000000000 | bytes 8000000 | tf_op jit(solution)/shard_map/earlier/pallas_call | solution.py:351
  (3 shorter events, 0.0 us)
Async XLA Ops:
  0.6 6.9 %collective-permute-start.1 = (f32[32,512]{1,0:T(8,128)}, f32[32,512]{1,0:T(8,128)S(1)}, u32[]{:S(2)}, u32[]{:S(2)}) collective-permute-start(f32[32,512]{1,0:T(8,128)} %param.6), channel_id=1, source_target_pairs={{1,2},{2,1},{5,6},{6,5},{9,10},{10,9},{13,14},{14,13},{17,18},{18,... | collective-permute-start | bytes 196616 | tf_op jit(solution)/shard_map/ppermute | solution.py:42
  2.1 5.5 %collective-permute-start = (f32[32,512]{1,0:T(8,128)}, f32[32,512]{1,0:T(8,128)S(1)}, u32[]{:S(2)}, u32[]{:S(2)}) collective-permute-start(f32[32,512]{1,0:T(8,128)} %param.6), channel_id=1, source_target_pairs={{0,1},{1,0},{2,3},{3,2},{4,5},{5,4},{6,7},{7,6},{8,9},{9,8},{10,11... | collective-permute-start | bytes 196616 | tf_op jit(solution)/shard_map/ppermute | solution.py:42
  6.5 1.1 %copy-start.1 = (f32[32,512]{1,0:T(8,128)S(1)}, f32[32,512]{1,0:T(8,128)}, u32[]{:S(2)}) copy-start(f32[32,512]{1,0:T(8,128)} %param.6) | copy-start | bytes 196612
  6.5 4.6 %copy-start = (f32[6,6,64,64]{3,2,1,0:T(8,128)S(1)}, f32[6,6,64,64]{3,2,1,0:T(8,128)}, u32[]{:S(2)}) copy-start(f32[6,6,64,64]{3,2,1,0:T(8,128)} %dw_ref.1) | copy-start | bytes 1769476
  7.6 12.4 %collective-permute-start.2 = (f32[64,256]{1,0:T(8,128)S(1)}, f32[64,256]{1,0:T(8,128)S(1)}, u32[]{:S(2)}, u32[]{:S(2)}) collective-permute-start(f32[64,256]{1,0:T(8,128)S(1)} %slice.20), channel_id=1, source_target_pairs={{0,4},{4,8},{8,12},{12,16},{16,20},{20,24},{24,28},{1,5},{5,9},{9,... | collective-permute-start | bytes 196616 | tf_op jit(solution)/shard_map/ppermute | solution.py:37

commit v4 on v3

--- a/solution.py
+++ b/solution.py
@@ -19,6 +19,7 @@
 LATER = ((64, 320), (64, 320), (64, 320), (64, 320), (80, 320), (96, 320), (128, 320))
 EARLIER = ((0, 80), (0, 80), (0, 80), (0, 80), (0, 80), (16, 96), (48, 128))
 CHUNK = 16
+OWN = ((4, 10), (4, 9))
 SLOTS = 32
 HIST = 256
 EDGE = 16
@@ -31,15 +32,15 @@
     return hi, (x - hi.astype(F32)).astype(BF)
 
 
-def from_behind(block, axis, distance):
-    devices = range(lax.axis_size(axis))
-    route = [(i - distance, i) for i in devices if i - distance in devices]
-    return lax.ppermute(block, axis, route)
+def from_behind(block, axis):
+    count = lax.axis_size(axis)
+    return lax.ppermute(block, axis, [(i, (i + 1) % count) for i in range(count)])
 
 
 def exchange(block, axis, first):
-    lows = range(first, lax.axis_size(axis) - 1, 2)
-    return lax.ppermute(block, axis, [p for i in lows for p in ((i, i + 1), (i + 1, i))])
+    count = lax.axis_size(axis)
+    swaps = [(i, (i + 1) % count) for i in range(first, count, 2)]
+    return lax.ppermute(block, axis, [p for i, j in swaps for p in ((i, j), (j, i))])
 
 
 def encoder_weights(small_ref, enc_ref, wide):
@@ -113,14 +114,15 @@
         parts[g, 0, begin : begin + count], parts[g, 1, begin : begin + count] = split(jnp.concatenate(rolled, 1))
 
 
-def network(ranges, parts, hid, top, low, mask, bias, enc_ref, dil_ref, dec_ref, encodes, group, ahead, kept, finished):
+def network(ranges, parts, hid, top, low, mask, bias, enc_ref, dil_ref, dec_ref, plan, group, ahead, kept, finished):
     eb = bias[0:1]
     low_half = lax.broadcasted_iota(jnp.int32, (1, 128), 1) < F
     m_time = jnp.where(lax.axis_index("tm") == 0, 0.0, 1.0).astype(F32)
 
     def keep(buf, i, value, layer):
         start, end = ranges[layer]
-        value = value * mask[layer, i : i + 1, :]
+        if mask is not None:
+            value = value * mask[layer, i : i + 1, :]
         if start < HH:
             value = jnp.concatenate([value[: HH - start] * m_time, value[HH - start :]], 0)
         hid[buf, i, start:end] = value
@@ -206,12 +208,12 @@
 
         return mm, finish
 
-    tasks = [encode(range(g, g + encodes)) for g in range(0, 8, encodes)]
-    for layer in range(LAYERS):
-        count = PAIRS - 1 - layer
-        tasks += [dilated(layer, range(i, min(i + group, count))) for i in range(0, count, group)]
+    tasks = [encode(groups) for groups in plan[0]]
+    for layer, pairs in enumerate(plan[1:]):
+        tasks += [dilated(layer, pairs[i : i + group]) for i in range(0, len(pairs), group)]
         tasks.append(lambda layer=layer: ahead(layer))
-    tasks.append(decode())
+    if len(plan) > LAYERS:
+        tasks.append(decode())
 
     def run(*refs):
         sets = [[refs[(2 * s + n) * SLOTS : (2 * s + n + 1) * SLOTS] for n in range(2)] for s in range(2)]
@@ -220,7 +222,7 @@
             if callable(task):
                 task()
                 continue
-            if task is tasks[-1] and waiting:
+            if len(plan) > LAYERS and task is tasks[-1] and waiting:
                 waiting()
                 waiting = None
             mm, finish = task
@@ -234,13 +236,45 @@
     pl.run_scoped(run, *[pltpu.ACC(n)((CHUNK, 256), F32) for s in range(2) for n in range(2) for k in range(SLOTS)])
 
 
-def later(s_ref, small_ref, dw_ref, enc_ref, sums_ref, h4_ref, h5_ref, dil_ref, dec_ref, st, hid, top, low, mask, parts, wide):
+def all_pairs(layer):
+    return tuple(range(PAIRS - 1 - layer))
+
+
+def own(sig_ref, small_ref, dw_ref, enc_ref, h0_ref, h1_ref, st, hid, top, low, parts, dil_ref):
+    small = small_ref[...]
+    bias = jnp.concatenate([small[18:25], small[18:25]], 1) * 0.5
+    layer_weights(0, dw_ref, dil_ref)
+    st[HIST - 8 : HIST, :] = jnp.zeros((8, 128), F32)
+    none = jnp.zeros((EDGE, 2 * HB), F32)
+    gather_taps(jnp.concatenate([none, sig_ref[...], none], 0), st, HIST, HH, HB, parts, 1)
+
+    def kept(layer, i, value):
+        if layer == 1:
+            h1_ref[i - OWN[1][0]] = value
+        elif i in (OWN[0][0], OWN[0][1] - 1):
+            h0_ref[0 if i == OWN[0][0] else 1] = value
+
+    plan = (tuple((g,) for g in range(OWN[0][0] // 2, OWN[0][1] // 2)), tuple(range(*OWN[1])))
+    network(LATER, parts, hid, top, low, None, bias, enc_ref, dil_ref, None, plan, 2, lambda layer: None, kept, None)
+
+
+def later(s_ref, small_ref, dw_ref, enc_ref, h0_ref, h1_ref, sums_ref, h4_ref, h5_ref, dil_ref, dec_ref, st, hid, top, low, mask, parts, wide):
     small = small_ref[...]
     bias = jnp.concatenate([small[18:25], small[18:25]], 1) * 0.5
     layer_weights(0, dw_ref, dil_ref)
     edge_masks(mask)
     st[HIST - 8 : HIST, :] = jnp.zeros((8, 128), F32)
     gather_taps(s_ref[...], st, HIST, HH, HB, parts, 1)
+    done = [(0, OWN[0][0], h0_ref, 0), (0, OWN[0][1] - 1, h0_ref, 1)]
+    done += [(1, i, h1_ref, i - OWN[1][0]) for i in range(*OWN[1])]
+    for layer, i, ref, k in done:
+        rows = slice(*LATER[layer])
+        value = ref[k]
+        hid[layer, i, rows] = value
+        top[layer, i, rows], low[layer, i, rows] = split(value)
+    plan = [[(g,) for g in range(8) if not OWN[0][0] <= 2 * g < OWN[0][1]]]
+    plan += [all_pairs(layer) for layer in range(LAYERS)]
+    plan[1] = tuple(i for i in plan[1] if not OWN[1][0] <= i < OWN[1][1])
 
     def ahead(layer):
         if layer + 1 < LAYERS:
@@ -257,7 +291,7 @@
     def finished(sums):
         sums_ref[...] = sums
 
-    network(LATER, parts, hid, top, low, mask, bias, enc_ref, dil_ref, dec_ref, 1, 3, ahead, kept, finished)
+    network(LATER, parts, hid, top, low, mask, bias, enc_ref, dil_ref, dec_ref, plan, 2, ahead, kept, finished)
 
 
 def earlier(s_ref, hist_ref, small_ref, enc_ref, sums_ref, h4_ref, h5_ref, dil_ref, dec_ref,
@@ -265,7 +299,8 @@
     small = small_ref[...]
     bias = jnp.concatenate([small[18:25], small[18:25]], 1) * 0.5
     edge_masks(mask)
-    gather_taps(jnp.concatenate([hist_ref[...], s_ref[:, :128]], 1), st, 0, 0, EARLIER[0][1], parts, 8)
+    hist = jnp.where(lax.axis_index("tm") == 0, 0.0, hist_ref[...])
+    gather_taps(jnp.concatenate([hist, s_ref[:, :128]], 1), st, 0, 0, EARLIER[0][1], parts, 8)
     for buf, ref, begin, end in ((0, h4_ref, 80, 96), (1, h5_ref, 96, 128)):
         for i in range(ref.shape[0]):
             value = ref[i]
@@ -295,7 +330,8 @@
     def finished(value):
         whole[: EARLIER[LAYERS][1] - base, :] = value
 
-    network(EARLIER, parts, hid, top, low, mask, bias, enc_ref, dil_ref, dec_ref, 4, 4, ahead,
+    plan = [[tuple(range(4)), tuple(range(4, 8))]] + [all_pairs(layer) for layer in range(LAYERS)]
+    network(EARLIER, parts, hid, top, low, mask, bias, enc_ref, dil_ref, dec_ref, plan, 4, ahead,
             lambda layer, i, value: None, finished)
     scores((0, 1))
 
@@ -306,32 +342,47 @@
     small = jnp.concatenate(
         [encode_weight.T, decode_weight, encode_bias.reshape(1, F), dilated_bias], 0
     )
-    own, small = lax.optimization_barrier((signal, small))
-    near = exchange(own, "fiber", 0)
+    signal, small = lax.optimization_barrier((signal, small))
+    near = exchange(signal, "fiber", 0)
     enc = pl.pallas_call(
         encoder_weights,
         out_shape=jax.ShapeDtypeStruct((8, 2, 256, 256), BF),
         in_specs=[vmem],
         out_specs=vmem,
         scratch_shapes=[pltpu.VMEM((3, 16, 256), F32)],
-        cost_estimate=pl.CostEstimate(flops=10**9, bytes_accessed=2 * 10**6, transcendentals=0),
+        cost_estimate=pl.CostEstimate(flops=10**6, bytes_accessed=2 * 10**6, transcendentals=0),
         compiler_params=pltpu.CompilerParams(vmem_limit_bytes=16 * 2**20),
         name="encoder_weights",
     )(small)
-    near, far, enc = lax.optimization_barrier((near, far, enc))
-    even = lax.axis_index("fiber") % 2 == 0
-    below = jnp.where(even, far[2 * CB - EDGE :], near[2 * CB - EDGE :])
-    above = jnp.where(even, near[:EDGE], far[:EDGE])
-    section = jnp.concatenate([below, signal, above], 0)
-    history = from_behind(section[:, 2 * HB - HIST :], "tm", 1)
     scratch = [
         pltpu.VMEM((HIST + 2 * HB, 128), F32),
         pltpu.VMEM((2, 16, ROWS, 128), F32),
         pltpu.VMEM((2, 16, ROWS, 128), BF),
         pltpu.VMEM((2, 16, ROWS, 128), BF),
-        pltpu.VMEM((LAYERS + 1, 16, 128), F32),
     ]
     params = pltpu.CompilerParams(vmem_limit_bytes=32 * 2**20)
+    h0, h1 = pl.pallas_call(
+        own,
+        out_shape=(
+            jax.ShapeDtypeStruct((2, HB, 128), F32),
+            jax.ShapeDtypeStruct((OWN[1][1] - OWN[1][0], HB, 128), F32),
+        ),
+        in_specs=[vmem] * 4,
+        out_specs=(vmem,) * 2,
+        scratch_shapes=scratch + [pltpu.VMEM((1, 2, ROWS, 256), BF), pltpu.VMEM((1, 2, 256, 256), BF)],
+        cost_estimate=pl.CostEstimate(flops=10**9, bytes_accessed=2 * 10**6, transcendentals=0),
+        compiler_params=params,
+        name="own",
+    )(signal, small, dilated_weight, enc)
+    near, far, h0, h1 = lax.optimization_barrier((near, far, h0, h1))
+    even = lax.axis_index("fiber") % 2 == 0
+    first = lax.axis_index("fiber") == 0
+    last = lax.axis_index("fiber") == lax.axis_size("fiber") - 1
+    below = jnp.where(first, 0.0, jnp.where(even, far[2 * CB - EDGE :], near[2 * CB - EDGE :]))
+    above = jnp.where(last, 0.0, jnp.where(even, near[:EDGE], far[:EDGE]))
+    section = jnp.concatenate([below, signal, above], 0)
+    history = from_behind(section[:, 2 * HB - HIST :], "tm")
+    scratch = scratch + [pltpu.VMEM((LAYERS + 1, 16, 128), F32)]
     sums, h4, h5, dil, dec = pl.pallas_call(
         later,
         out_shape=(
@@ -341,13 +392,13 @@
             jax.ShapeDtypeStruct((LAYERS, 2, 256, 256), BF),
             jax.ShapeDtypeStruct((5, 256, 256), BF),
         ),
-        in_specs=[vmem] * 4,
+        in_specs=[vmem] * 6,
         out_specs=(vmem,) * 5,
         scratch_shapes=scratch + [pltpu.VMEM((1, 2, ROWS, 256), BF), pltpu.VMEM((5, 128, 256), F32)],
         cost_estimate=pl.CostEstimate(flops=8 * 10**9, bytes_accessed=8 * 10**6, transcendentals=0),
         compiler_params=params,
         name="later",
-    )(section, small, dilated_weight, enc)
+    )(section, small, dilated_weight, enc, h0, h1)
     return pl.pallas_call(
         earlier,
         out_shape=(

time: 24.6 us -> 20.9 us (0.85)
  starting transfers between devices: 8.46 us -> 5.43 us
  waiting for transfers between devices: 0.96 us -> 0.01 us
  Pallas kernels: 13.4 us -> 13.7 us
    ppermute x3, starting transfers between devices: 8.46 us -> 5.43 us  [the longest x2 3.21 us: exchange(): lax.ppermute(block, axis, [p for i, j in swaps for p in ((i, j), (j, i))])]
    pallas_call x0 -> x1, Pallas kernels: none -> 1.17 us  [on_device(): pl.pallas_call(own, out_shape=(jax.ShapeDtypeStruct((2, HB, 128), F32), j...]
    ppermute x3, waiting for transfers between devices: 0.96 us -> 0.01 us  [the longest x2 0.01 us: exchange(): lax.ppermute(block, axis, [p for i, j in swaps for p in ((i, j), (j, i))])]
    pallas_call x1, Pallas kernels: 8.93 us -> 8.06 us  [on_device(): pl.pallas_call(later, out_shape=(jax.ShapeDtypeStruct((LATER[LAYERS][1] -...]
  transfers between devices with their start and end apart: 3 -> 3, of which waited for: 1 -> 0; matrix products, arithmetic and copies ran while one was open for 3% -> 4% of each run, Pallas kernels for 37% -> 45%
where the time goes in v4:
time: 20.9 us; the launch traced here: 20.7 us
  Pallas kernels  13.7 us (66%)
  starting transfers between devices  5.43 us (26%)
  other arithmetic  0.78 us (4%)
  between operations  0.73 us (3%)
    pallas_call x1, Pallas kernels, on_device(): pl.pallas_call(later, out_shape=(jax.ShapeDtypeStruct((LATER[LAYERS][1] -...  8.06 us
    pallas_call x1, Pallas kernels, on_device(): pl.pallas_call(earlier, out_shape=(jax.ShapeDtypeStruct((2 * CB, 2 * HB),...  4.37 us
    ppermute x2, starting transfers between devices, exchange(): lax.ppermute(block, axis, [p for i, j in swaps for p in ((i, j), (j, i))])  3.21 us
    ppermute x1, starting transfers between devices, from_behind(): lax.ppermute(block, axis, [(i, (i + 1) % count) for i in range(count)])  2.22 us
    pallas_call x1, Pallas kernels, on_device(): pl.pallas_call(own, out_shape=(jax.ShapeDtypeStruct((2, HB, 128), F32), j...  1.17 us
    concatenate x1, other arithmetic, on_device(): jnp.concatenate([encode_weight.T, decode_weight, encode_bias.reshape(1, F...  0.76 us
  transfers between devices with their start and end apart: 3, of which 0 were waited for; matrix products, arithmetic and copies ran while one was open for 4% of the time, Pallas kernels for 45%

profile of v4, /device:TPU:0, one launch (start us, length us, event | category | flops | bytes accessed | tf_op | source)
XLA Modules:
  0.0 20.7 jit_solution(223172673037485172)
XLA Ops:
  0.6 0.0 copy-start
  0.6 0.0 copy-start.1
  0.7 2.5 %collective-permute-start.1 = (f32[32,512]{1,0:T(8,128)}, f32[32,512]{1,0:T(8,128)S(1)}, u32[]{:S(2)}, u32[]{:S(2)}) collective-permute-start(f32[32,512]{1,0:T(8,128)} %sig_ref), channel_id=1, source_target_pairs={{1,2},{2,1},{3,0},{0,3},{5,6},{6,5},{7,4},{4,7},{9,10},{10,9},{11,... | collective-permute-start | bytes 196616 | tf_op jit(solution)/shard_map/ppermute | solution.py:43
  3.1 0.8 %pad_maximum_fusion.1.small_ref = f32[25,64]{1,0:T(8,128)S(1)} fusion(f32[6,64]{1,0:T(8,128)} %param.10, f32[1,64]{1,0:T(1,128)} %bitcast.3, f32[9,64]{1,0:T(8,128)} %param.11, f32[9,64]{1,0:T(8,128)} %bitcast.2), kind=kLoop, calls=%fused_computation.3 | loop fusion | flops 4800 | bytes 12800 | tf_op jit(solution)/shard_map/concatenate | solution.py:342
  3.9 0.7 %collective-permute-start = (f32[32,512]{1,0:T(8,128)}, f32[32,512]{1,0:T(8,128)S(1)}, u32[]{:S(2)}, u32[]{:S(2)}) collective-permute-start(f32[32,512]{1,0:T(8,128)} %sig_ref), channel_id=1, source_target_pairs={{0,1},{1,0},{2,3},{3,2},{4,5},{5,4},{6,7},{7,6},{8,9},{9,8},{10,11... | collective-permute-start | bytes 196616 | tf_op jit(solution)/shard_map/ppermute | solution.py:43
  4.6 0.2 encoder_weights.1.enc_ref
  4.8 0.0 copy-done
  4.8 0.0 copy-done.1
  4.8 1.2 %own.1 = (f32[2,256,128]{2,1,0:T(8,128)S(1)}, f32[5,256,128]{2,1,0:T(8,128)S(1)}) custom-call(f32[32,512]{1,0:T(8,128)S(1)} %copy-done, f32[25,64]{1,0:T(8,128)S(1)} %pad_maximum_fusion.1.small_ref, f32[6,6,64,64]{3,2,1,0:T(8,128)S(1)} %copy-done.1, bf16[8,2,256,256]{3,2,1,0:T(8,128)(2,1)S(1)} %encoder_weights.1.enc_ref), custom_call_target="tpu_custom_call" | custom-call | flops 1000000000 | bytes 2000000 | tf_op jit(solution)/shard_map/own/pallas_call | solution.py:364
  6.0 0.0 collective-permute-done
  6.0 0.0 collective-permute-done.1
  6.1 2.2 %collective-permute-start.2 = (f32[64,256]{1,0:T(8,128)S(1)}, f32[64,256]{1,0:T(8,128)S(1)}, u32[]{:S(2)}, u32[]{:S(2)}) collective-permute-start(f32[64,256]{1,0:T(8,128)S(1)} %slice.20), channel_id=1, source_target_pairs={{0,4},{4,8},{8,12},{12,16},{16,20},{20,24},{24,28},{28,0},{1,5},{5... | collective-permute-start | bytes 196616 | tf_op jit(solution)/shard_map/ppermute | solution.py:37
  8.3 8.1 %later.1 = (f32[192,128]{1,0:T(8,128)S(1)}, f32[11,16,128]{2,1,0:T(8,128)S(1)}, f32[10,32,128]{2,1,0:T(8,128)S(1)}, bf16[6,2,256,256]{3,2,1,0:T(8,128)(2,1)S(1)}, bf16[5,256,256]{2,1,0:T(8,128)(2,1)S(1)}) custom-call(f32[64,512]{1,0:T(8,128)S(1)} %pad_maximum_fusion.s_ref, f32[25,64]{1,0:T(8,128)S(1)} %pad_maximum_fusion.1.small_ref, ...), custom_call_target="tpu_custom_call" | custom-call | flops 8000000000 | bytes 8000000 | tf_op jit(solution)/shard_map/later/pallas_call | solution.py:386
  16.3 0.0 collective-permute-done.2.hist_ref
  16.4 4.4 %earlier.1 = (f32[32,512]{1,0:T(8,128)}, f32[2,4]{1,0:T(2,128)}) custom-call(f32[64,512]{1,0:T(8,128)S(1)} %pad_maximum_fusion.s_ref, f32[64,256]{1,0:T(8,128)S(1)} %collective-permute-done.2.hist_ref, f32[25,64]{1,0:T(8,128)S(1)} %pad_maximum_fusion.1.small_ref, bf16[8,2,256,256]{3,2,1,0:T(8,128)(2,1)S(1)} %encoder_weights.1.enc_ref, ...), custom_call_target="tpu_custom_call" | custom-call | flops 2000000000 | bytes 8000000 | tf_op jit(solution)/shard_map/earlier/pallas_call | solution.py:402
  (3 shorter events, 0.0 us)
Async XLA Ops:
  0.6 4.2 %copy-start = (f32[32,512]{1,0:T(8,128)S(1)}, f32[32,512]{1,0:T(8,128)}, u32[]{:S(2)}) copy-start(f32[32,512]{1,0:T(8,128)} %sig_ref) | copy-start | bytes 196612
  0.6 4.2 %copy-start.1 = (f32[6,6,64,64]{3,2,1,0:T(8,128)S(1)}, f32[6,6,64,64]{3,2,1,0:T(8,128)}, u32[]{:S(2)}) copy-start(f32[6,6,64,64]{3,2,1,0:T(8,128)} %dw_ref.3) | copy-start | bytes 1769476
  0.7 5.3 %collective-permute-start.1 = (f32[32,512]{1,0:T(8,128)}, f32[32,512]{1,0:T(8,128)S(1)}, u32[]{:S(2)}, u32[]{:S(2)}) collective-permute-start(f32[32,512]{1,0:T(8,128)} %sig_ref), channel_id=1, source_target_pairs={{1,2},{2,1},{3,0},{0,3},{5,6},{6,5},{7,4},{4,7},{9,10},{10,9},{11,... | collective-permute-start | bytes 196616 | tf_op jit(solution)/shard_map/ppermute | solution.py:43
  3.9 2.1 %collective-permute-start = (f32[32,512]{1,0:T(8,128)}, f32[32,512]{1,0:T(8,128)S(1)}, u32[]{:S(2)}, u32[]{:S(2)}) collective-permute-start(f32[32,512]{1,0:T(8,128)} %sig_ref), channel_id=1, source_target_pairs={{0,1},{1,0},{2,3},{3,2},{4,5},{5,4},{6,7},{7,6},{8,9},{9,8},{10,11... | collective-permute-start | bytes 196616 | tf_op jit(solution)/shard_map/ppermute | solution.py:43
  6.1 10.3 %collective-permute-start.2 = (f32[64,256]{1,0:T(8,128)S(1)}, f32[64,256]{1,0:T(8,128)S(1)}, u32[]{:S(2)}, u32[]{:S(2)}) collective-permute-start(f32[64,256]{1,0:T(8,128)S(1)} %slice.20), channel_id=1, source_target_pairs={{0,4},{4,8},{8,12},{12,16},{16,20},{20,24},{24,28},{28,0},{1,5},{5... | collective-permute-start | bytes 196616 | tf_op jit(solution)/shard_map/ppermute | solution.py:37

commit v5 on v4

v5 whole, which is shorter than its diff:
```python
import functools

import jax
import jax.numpy as jnp
from jax import lax
from jax.experimental import pallas as pl
from jax.experimental.pallas import tpu as pltpu
from jax.sharding import PartitionSpec as P

LAYERS = 6
F = 64
TILE_C = 16
TILE_T = 128
CB = 16
HB = 256
HH = 64
ROWS = HH + HB
PAIRS = (CB + 2 * LAYERS + 2) // 2
LATER = ((64, 320), (64, 320), (64, 320), (64, 320), (80, 320), (96, 320), (128, 320))
EARLIER = ((0, 80), (0, 80), (0, 80), (0, 80), (0, 80), (16, 96), (48, 128))
CHUNK = 16
OWN = ((4, 10), (4, 9), (4, 8))
SLOTS = 32
HIST = 256
EDGE = 16
BF = jnp.bfloat16
F32 = jnp.float32


def split(x):
    hi = x.astype(BF)
    return hi, (x - hi.astype(F32)).astype(BF)


def from_behind(block, axis):
    count = lax.axis_size(axis)
    return lax.ppermute(block, axis, [(i, (i + 1) % count) for i in range(count)])


def exchange(block, first):
    times, count = lax.axis_size("tm"), lax.axis_size("fiber")
    swaps = [(t * count + i, t * count + i + 1) for t in range(times) for i in range(first, count - 1, 2)]
    if first:
        swaps += [(t * count + i, (t + 1) * count + i) for t in range(0, times, 2) for i in (0, count - 1)]
    return lax.ppermute(block, ("tm", "fiber"), [p for i, j in swaps for p in ((i, j), (j, i))])


def encoder_weights(small_ref, enc_ref, wide):
    ew = small_ref[0:9] * 0.5
    wide[...] = jnp.zeros(wide.shape, F32)
    for j in range(4):
        for a in range(3):
            for b in range(3):
                wide[b, 3 + 2 * j + a : 4 + 2 * j + a, j * F : j * F + F] = ew[3 * a + b : 3 * a + b + 1, :]
    none = jnp.zeros((F, 256), F32)
    for g in range(8):
        parts = []
        for b in range(3):
            piece = wide[b]
            if g < 7:
                rows = [none[: 8 * g], piece, none[: F - 16 - 8 * g]]
            else:
                rows = [none[: F - 8], piece[:8]]
            parts += [r for r in rows if r.shape[0]]
        parts.append(none)
        enc_ref[g, 0], enc_ref[g, 1] = split(jnp.concatenate(parts, 0))


def layer_weights(layer, dw_ref, dil_ref):
    zero = jnp.zeros((F, F), F32)
    ins = (1, 0, 3, 2) if layer % 2 else (0, 1, 2, 3)
    outs = (1, 2) if layer % 2 else (2, 1)
    rows = []
    for lag in range(2):
        for co in outs:
            cols = [
                dw_ref[layer, 2 * (ci - co + 1) + lag] * 0.5 if 0 <= ci - co + 1 <= 2 else zero
                for ci in ins
            ]
            rows.append(jnp.concatenate(cols, 1))
    dil_ref[layer, 0], dil_ref[layer, 1] = split(jnp.concatenate(rows, 0).T)


def decoder_weights(de, dec_ref, wide):
    wide[...] = jnp.zeros(wide.shape, F32)
    for c in range(CB + 1):
        for a in range(3):
            p = 2 * c + a - 1
            if 0 <= p < 2 * CB:
                for b in range(3):
                    k, at = c % 4 * F, b * 2 * CB + p
                    wide[c // 4, at : at + 1, k : k + F] = de[3 * a + b : 3 * a + b + 1, :]
    for q in range(5):
        hi, lo = split(wide[q].T)
        dec_ref[q] = jnp.concatenate([hi, lo], 1)


def edge_masks(mask):
    m_low = jnp.where(lax.axis_index("fiber") == 0, 0.0, 1.0).astype(F32)
    m_high = jnp.where(lax.axis_index("fiber") == lax.axis_size("fiber") - 1, 0.0, 1.0).astype(F32)
    pair = lax.broadcasted_iota(jnp.int32, (16, 128), 0)
    lane = lax.broadcasted_iota(jnp.int32, (16, 128), 1)
    for layer in range(LAYERS + 1):
        second = lane // F if layer % 2 == 0 else 1 - lane // F
        c = layer - LAYERS + 2 * pair + second
        mask[layer] = jnp.where(c < 0, m_low, jnp.where(c >= CB, m_high, 1.0))


def gather_taps(s, st, first, begin, count, parts, groups):
    both = jnp.concatenate([s, pltpu.roll(s, 1, 1)], 0)
    for n in range(s.shape[1] // 128):
        st[pl.ds(first + n * 128, 128), :] = both[:, n * 128 : n * 128 + 128].T
    x = [st[pl.ds(HIST + 2 * (begin - HH) - back, count, 2), :] for back in (0, 2)]
    for g in range(groups):
        rolled = [pltpu.roll(half, 128 - 8 * g, 1) if g else half for half in x]
        parts[g, 0, begin : begin + count], parts[g, 1, begin : begin + count] = split(jnp.concatenate(rolled, 1))


def network(tasks_of, parts, hid, top, low, mask, bias, enc_ref, dil_ref, dec_ref, kept):
    eb = bias[0:1]
    low_half = lax.broadcasted_iota(jnp.int32, (1, 128), 1) < F
    sublane = lax.broadcasted_iota(jnp.int32, (8, 128), 0)
    m_time = jnp.where(lax.axis_index("tm") == 0, 0.0, 1.0).astype(F32)

    def keep(buf, i, value, layer, r, scale):
        if scale is not None:
            value = value * scale
        if r < HH:
            value = value * m_time
        hid[buf, i, r : r + CHUNK] = value
        top[buf, i, r : r + CHUNK], low[buf, i, r : r + CHUNK] = split(value)
        kept(layer, i, value, r)

    def scale_of(layer, i):
        return None if mask is None else mask[layer, i : i + 1, :]

    def chunks(pairs, begin, end):
        units = [(i, r) for i in pairs for r in range(begin, end, CHUNK)]
        half = (len(units) + 1) // 2
        return units[:half], units[half:]

    def multiply(acc, units, piece, steps):
        for step, weights in enumerate(steps):
            for n in range(2):
                for k, matrix in enumerate(weights):
                    pltpu.matmul_push_rhs(matrix, k, n)
            for part, load in ((0, 0), (1, None), (0, 1))[: len(weights) + 1]:
                for n in range(2):
                    for slot, unit in enumerate(units[n]):
                        pltpu.matmul_acc_lhs(acc[n][slot], piece(part, step, unit), load if slot == 0 else None)

    def each(acc, units, i):
        for n in range(2):
            for slot, unit in enumerate(units[n]):
                if unit[0] == i:
                    yield unit[1], pltpu.matmul_pop(acc[n][slot])

    def encode(ranges, groups):
        units = chunks(groups, *ranges[0])

        def mm(acc):
            g, same = (0, parts.shape[0] == 1) if len(groups) > 1 else (groups[0], True)
            multiply(acc, units, lambda part, step, unit: parts[0 if same else unit[0], part, unit[1] : unit[1] + CHUNK],
                     ((enc_ref[g, 0], enc_ref[g, 1]),))

        def finish(acc):
            for g in groups:
                scales = [scale_of(0, 2 * g + n) for n in range(2)]
                for r, y in each(acc, units, g):
                    for n in range(2):
                        if 2 * g + n < PAIRS:
                            u = y[:, n * 128 : n * 128 + 128] + eb
                            keep(0, 2 * g + n, u + u * jnp.tanh(u), 0, r, scales[n])

        return mm, finish

    def dilated(ranges, layer, pairs):
        d = 2**layer
        src, dst = layer % 2, 1 - layer % 2
        start, end = ranges[layer + 1]
        begin = max(ranges[layer][0], (start - d) // CHUNK * CHUNK)
        units = chunks(pairs, begin, end)

        def piece(part, step, unit):
            i, r = unit
            ref = low if part else top
            return jnp.concatenate([ref[src, i, r : r + CHUNK], ref[src, i + 1, r : r + CHUNK]], 1)

        def mm(acc):
            multiply(acc, units, piece, ((dil_ref[layer, 0], dil_ref[layer, 1]),))

        def finish(acc):
            for i in pairs:
                near, far = (i, i + 1) if src else (i + 1, i)
                scale = scale_of(layer + 1, i)
                lagged = {}
                for r, y in each(acc, units, i):
                    for k in range(0, CHUNK, 8):
                        lagged[r + k] = y[k : k + 8, 128:]
                        if d < 8:
                            lagged[r + k] = pltpu.roll(lagged[r + k], d, 0)
                    if r < start:
                        continue
                    past = []
                    for k in range(r, r + CHUNK, 8):
                        if d < 8:
                            past.append(jnp.where(sublane < d, lagged.get(k - 8, lagged[k]), lagged[k]))
                        else:
                            past.append(lagged.get(k - d, lagged[k]))
                    u = y[:, :128] + jnp.concatenate(past, 0) + bias[layer + 1 : layer + 2]
                    rows = slice(r, r + CHUNK)
                    h = jnp.where(low_half, hid[src, near, rows], hid[src, far, rows])
                    keep(dst, i, h + u + u * jnp.tanh(u), layer + 1, r, scale)

        return mm, finish

    def decode(ranges, finished):
        units = chunks((0,), *ranges[LAYERS])

        def piece(part, step, unit):
            ref, r = low if part else top, unit[1]
            return jnp.concatenate([ref[0, i, r : r + CHUNK] for i in (2 * step, min(2 * step + 1, 8))], 1)

        def mm(acc):
            multiply(acc, units, piece, [(dec_ref[q],) for q in range(5)])

        def finish(acc):
            for r, y in each(acc, units, 0):
                finished(r, y[:, :128] + y[:, 128:])

        return mm, finish

    tasks = tasks_of(encode, dilated, decode)

    def run(*refs):
        sets = [[refs[(2 * s + n) * SLOTS : (2 * s + n + 1) * SLOTS] for n in range(2)] for s in range(2)]
        waiting, turn = None, 0
        for task in tasks:
            if callable(task):
                task()
                continue
            if task is None:
                if waiting:
                    waiting()
                waiting = None
                continue
            mm, finish = task
            mm(sets[turn])
            if waiting:
                waiting()
            waiting = functools.partial(finish, sets[turn])
            turn = 1 - turn
        if waiting:
            waiting()

    pl.run_scoped(run, *[pltpu.ACC(n)((CHUNK, 256), F32) for s in range(2) for n in range(2) for k in range(SLOTS)])


def all_pairs(layer, group):
    pairs = tuple(range(PAIRS - 1 - layer))
    return [pairs[i : i + group] for i in range(0, len(pairs), group)]


def handed(layer):
    pairs = range(*OWN[layer])
    return list(pairs) if layer == len(OWN) - 1 else [pairs[0], pairs[-1]]


def own(sig_ref, small_ref, dw_ref, enc_ref, *refs):
    outs = refs[: len(OWN)]
    st, hid, top, low, parts, dil_ref = refs[len(OWN) :]
    small = small_ref[...]
    bias = jnp.concatenate([small[18:25], small[18:25]], 1) * 0.5
    st[HIST - 8 : HIST, :] = jnp.zeros((8, 128), F32)
    none = jnp.zeros((EDGE, 2 * HB), F32)
    gather_taps(jnp.concatenate([none, sig_ref[...], none], 0), st, HIST, HH, HB, parts, 1)
    for layer in range(len(OWN) - 1):
        layer_weights(layer, dw_ref, dil_ref)

    def kept(layer, i, value, r):
        if i in handed(layer):
            at = r - LATER[layer][0]
            outs[layer][handed(layer).index(i), at : at + CHUNK] = value

    def tasks(encode, dilated, decode):
        out = [encode(LATER, (g,)) for g in range(OWN[0][0] // 2, OWN[0][1] // 2)]
        for layer in range(len(OWN) - 1):
            pairs = tuple(range(*OWN[layer + 1]))
            out += [dilated(LATER, layer, group) for group in (pairs[:2], *zip(pairs[2:]))]
        return out

    network(tasks, parts, hid, top, low, None, bias, enc_ref, dil_ref, None, kept)


def later(s_ref, small_ref, dw_ref, enc_ref, *refs):
    done = refs[: len(OWN)]
    sums_ref, h4_ref, h5_ref, dil_ref, dec_ref, st, hid, top, low, mask, parts, wide = refs[len(OWN) :]
    small = small_ref[...]
    bias = jnp.concatenate([small[18:25], small[18:25]], 1) * 0.5
    layer_weights(0, dw_ref, dil_ref)
    edge_masks(mask)
    st[HIST - 8 : HIST, :] = jnp.zeros((8, 128), F32)
    gather_taps(s_ref[...], st, HIST, HH, HB, parts, 1)

    def fetch(layer):
        rows = slice(*LATER[layer])
        for k, i in enumerate(handed(layer)):
            value = done[layer][k]
            hid[layer % 2, i, rows] = value
            top[layer % 2, i, rows], low[layer % 2, i, rows] = split(value)

    def kept(layer, i, value, r):
        if layer == 4 and r < EARLIER[5][1]:
            h4_ref[i, r - LATER[4][0] : r - LATER[4][0] + CHUNK] = value
        if layer == 5 and r < EARLIER[6][1]:
            h5_ref[i, r - LATER[5][0] : r - LATER[5][0] + CHUNK] = value

    def store(r, value):
        sums_ref[r - LATER[LAYERS][0] : r - LATER[LAYERS][0] + CHUNK, :] = value

    def tasks(encode, dilated, decode):
        out = [functools.partial(fetch, 0), functools.partial(fetch, 1)]
        out += [encode(LATER, (g,)) for g in range(8) if not OWN[0][0] <= 2 * g < OWN[0][1]]
        for layer in range(LAYERS):
            pairs = [i for i in range(PAIRS - 1 - layer) if layer + 1 >= len(OWN) or i not in range(*OWN[layer + 1])]
            out += [dilated(LATER, layer, pairs[i : i + 2]) for i in range(0, len(pairs), 2)]
            if 2 <= layer + 2 < len(OWN):
                out += [None, functools.partial(fetch, layer + 2)]
            if layer + 1 < LAYERS:
                out.append(functools.partial(layer_weights, layer + 1, dw_ref, dil_ref))
            if layer == 2:
                out.append(lambda: decoder_weights(small[9:18], dec_ref, wide))
        return out + [None, decode(LATER, store)]

    network(tasks, parts, hid, top, low, mask, bias, enc_ref, dil_ref, dec_ref, kept)


def earlier(s_ref, hist_ref, small_ref, enc_ref, sums_ref, h4_ref, h5_ref, dil_ref, dec_ref,
            recon_ref, err_ref, st, hid, top, low, mask, parts, wide, whole):
    small = small_ref[...]
    bias = jnp.concatenate([small[18:25], small[18:25]], 1) * 0.5
    edge_masks(mask)
    hist = jnp.where(lax.axis_index("tm") == 0, 0.0, hist_ref[...])
    gather_taps(jnp.concatenate([hist, s_ref[:, :128]], 1), st, 0, 0, EARLIER[0][1], parts, 8)
    base = EARLIER[LAYERS][0]

    def fetch():
        for buf, ref, begin, end in ((0, h4_ref, 80, 96), (1, h5_ref, 96, 128)):
            for i in range(ref.shape[0]):
                value = ref[i]
                hid[buf, i, begin:end] = value
                top[buf, i, begin:end], low[buf, i, begin:end] = split(value)
        whole[LATER[LAYERS][0] - base :, :] = sums_ref[...]

    def scores(tiles):
        begin, count = HH - base + tiles[0] * TILE_T // 2, len(tiles) * TILE_T // 2
        now, past = whole[begin : begin + count, :], whole[begin - 1 : begin - 1 + count, :]
        wide[pl.ds(tiles[0] * TILE_T, count, 2), :] = now + pltpu.roll(past, 128 - 4 * CB, 1)
        wide[pl.ds(tiles[0] * TILE_T + 1, count, 2), :] = pltpu.roll(now, 128 - 2 * CB, 1)
        for n in tiles:
            cols = slice(n * TILE_T, n * TILE_T + TILE_T)
            out = wide[cols, :].T[: 2 * CB]
            recon_ref[:, cols] = out
            sq = (out - s_ref[EDGE : EDGE + 2 * CB, cols]) ** 2
            per = [jnp.sum(sq[m * TILE_C : m * TILE_C + TILE_C], keepdims=True) for m in range(2 * CB // TILE_C)]
            err_ref[:, n : n + 1] = jnp.concatenate(per, 0) * (1.0 / (TILE_C * TILE_T))

    def store(r, value):
        whole[r - base : r - base + CHUNK, :] = value

    def tasks(encode, dilated, decode):
        out = [encode(EARLIER, (0, 1, 2, 3)), encode(EARLIER, (4, 5, 6, 7)), fetch]
        for layer in range(LAYERS):
            out += [dilated(EARLIER, layer, pairs) for pairs in all_pairs(layer, 4)]
            if layer == 1:
                out.append(functools.partial(scores, (2, 3)))
        return out + [None, decode(EARLIER, store)]

    network(tasks, parts, hid, top, low, mask, bias, enc_ref, dil_ref, dec_ref, lambda layer, i, value, r: None)
    scores((0, 1))


def on_device(signal, encode_weight, encode_bias, dilated_weight, dilated_bias, decode_weight):
    vmem = pl.BlockSpec(memory_space=pltpu.VMEM)
    far = exchange(signal, 1)
    small = jnp.concatenate(
        [encode_weight.T, decode_weight, encode_bias.reshape(1, F), dilated_bias], 0
    )
    near = exchange(signal, 0)
    enc = pl.pallas_call(
        encoder_weights,
        out_shape=jax.ShapeDtypeStruct((8, 2, 256, 256), BF),
        in_specs=[vmem],
        out_specs=vmem,
        scratch_shapes=[pltpu.VMEM((3, 16, 256), F32)],
        cost_estimate=pl.CostEstimate(flops=10**6, bytes_accessed=2 * 10**6, transcendentals=0),
        compiler_params=pltpu.CompilerParams(vmem_limit_bytes=16 * 2**20),
        name="encoder_weights",
    )(small)
    scratch = [
        pltpu.VMEM((HIST + 2 * HB, 128), F32),
        pltpu.VMEM((2, 16, ROWS, 128), F32),
        pltpu.VMEM((2, 16, ROWS, 128), BF),
        pltpu.VMEM((2, 16, ROWS, 128), BF),
    ]
    params = pltpu.CompilerParams(vmem_limit_bytes=32 * 2**20)
    done = pl.pallas_call(
        own,
        out_shape=tuple(jax.ShapeDtypeStruct((len(handed(layer)), HB, 128), F32) for layer in range(len(OWN))),
        in_specs=[vmem] * 4,
        out_specs=(vmem,) * len(OWN),
        scratch_shapes=scratch
        + [pltpu.VMEM((1, 2, ROWS, 256), BF), pltpu.VMEM((len(OWN) - 1, 2, 256, 256), BF)],
        cost_estimate=pl.CostEstimate(flops=10**9, bytes_accessed=2 * 10**6, transcendentals=0),
        compiler_params=params,
        name="own",
    )(signal, small, dilated_weight, enc)
    near, far, *done = lax.optimization_barrier((near, far, *done))
    even = lax.axis_index("fiber") % 2 == 0
    first = lax.axis_index("fiber") == 0
    last = lax.axis_index("fiber") == lax.axis_size("fiber") - 1
    below = jnp.where(first, 0.0, jnp.where(even, far[2 * CB - EDGE :], near[2 * CB - EDGE :]))
    above = jnp.where(last, 0.0, jnp.where(even, near[:EDGE], far[:EDGE]))
    section = jnp.concatenate([below, signal, above], 0)
    history = from_behind(section[:, 2 * HB - HIST :], "tm")
    scratch = scratch + [pltpu.VMEM((LAYERS + 1, 16, 128), F32)]
    results = pl.pallas_call(
        later,
        out_shape=(
            jax.ShapeDtypeStruct((LATER[LAYERS][1] - LATER[LAYERS][0], 128), F32),
            jax.ShapeDtypeStruct((PAIRS - 4, EARLIER[5][1] - LATER[4][0], 128), F32),
            jax.ShapeDtypeStruct((PAIRS - 5, EARLIER[6][1] - LATER[5][0], 128), F32),
            jax.ShapeDtypeStruct((LAYERS, 2, 256, 256), BF),
            jax.ShapeDtypeStruct((5, 256, 256), BF),
        ),
        in_specs=[vmem] * (4 + len(OWN)),
        out_specs=(vmem,) * 5,
        scratch_shapes=scratch + [pltpu.VMEM((1, 2, ROWS, 256), BF), pltpu.VMEM((5, 128, 256), F32)],
        cost_estimate=pl.CostEstimate(flops=7 * 10**9, bytes_accessed=8 * 10**6, transcendentals=0),
        compiler_params=params,
        name="later",
    )(section, small, dilated_weight, enc, *done)
    return pl.pallas_call(
        earlier,
        out_shape=(
            jax.ShapeDtypeStruct((2 * CB, 2 * HB), F32),
            jax.ShapeDtypeStruct((2 * CB // TILE_C, 2 * HB // TILE_T), F32),
        ),
        in_specs=[vmem] * 9,
        out_specs=(vmem,) * 2,
        scratch_shapes=scratch
        + [
            pltpu.VMEM((8, 2, EARLIER[0][1], 256), BF),
            pltpu.VMEM((2 * HB, 128), F32),
            pltpu.VMEM((ROWS - EARLIER[LAYERS][0], 128), F32),
        ],
        cost_estimate=pl.CostEstimate(flops=2 * 10**9, bytes_accessed=8 * 10**6, transcendentals=0),
        compiler_params=params,
        name="earlier",
    )(section, history, small, enc, *results)


def solution(mesh):
    return jax.shard_map(
        on_device,
        mesh=mesh,
        in_specs=(P("fiber", "tm"), P(), P(), P(), P(), P()),
        out_specs=(P("fiber", "tm"), P("fiber", "tm")),
        check_vma=False,
    )
```

time: 20.9 us -> 20.5 us (0.981)
  starting transfers between devices: 5.43 us -> 5 us
    pallas_call x1, Pallas kernels: 1.17 us -> 1.63 us  [on_device(): pl.pallas_call(own, out_shape=tuple((jax.ShapeDtypeStruct((len(handed(lay...]
    pallas_call x1, Pallas kernels: 8.06 us -> 7.67 us  [on_device(): pl.pallas_call(later, out_shape=(jax.ShapeDtypeStruct((LATER[LAYERS][1] -...]
    ppermute x1, starting transfers between devices: 2.22 us -> 1.92 us  [from_behind(): lax.ppermute(block, axis, [(i, (i + 1) % count) for i in range(count)])]
  transfers between devices with their start and end apart: 3 -> 3, of which waited for: 0 -> 0; matrix products, arithmetic and copies ran while one was open for 4% -> 4% of each run, Pallas kernels for 45% -> 46%
where the time goes in v5:
time: 20.5 us; the launch traced here: 20.4 us
  Pallas kernels  13.8 us (67%)
  starting transfers between devices  5 us (24%)
  other arithmetic  0.78 us (4%)
  between operations  0.74 us (4%)
    pallas_call x1, Pallas kernels, on_device(): pl.pallas_call(later, out_shape=(jax.ShapeDtypeStruct((LATER[LAYERS][1] -...  7.67 us
    pallas_call x1, Pallas kernels, on_device(): pl.pallas_call(earlier, out_shape=(jax.ShapeDtypeStruct((2 * CB, 2 * HB),...  4.37 us
    ppermute x2, starting transfers between devices, exchange(): lax.ppermute(block, ('tm', 'fiber'), [p for i, j in swaps for p in ((i, j...  3.08 us
    ppermute x1, starting transfers between devices, from_behind(): lax.ppermute(block, axis, [(i, (i + 1) % count) for i in range(count)])  1.92 us
    pallas_call x1, Pallas kernels, on_device(): pl.pallas_call(own, out_shape=tuple((jax.ShapeDtypeStruct((len(handed(lay...  1.63 us
    concatenate x1, other arithmetic, on_device(): jnp.concatenate([encode_weight.T, decode_weight, encode_bias.reshape(1, F...  0.76 us
  transfers between devices with their start and end apart: 3, of which 0 were waited for; matrix products, arithmetic and copies ran while one was open for 4% of the time, Pallas kernels for 46%

profile of v5, /device:TPU:0, one launch (start us, length us, event | category | flops | bytes accessed | tf_op | source)
XLA Modules:
  0.0 20.4 jit_solution(9610723687548814968)
XLA Ops:
  0.6 0.0 copy-start
  0.6 0.0 copy-start.1
  0.7 0.5 %collective-permute-start = (f32[32,512]{1,0:T(8,128)}, f32[32,512]{1,0:T(8,128)S(1)}, u32[]{:S(2)}, u32[]{:S(2)}) collective-permute-start(f32[32,512]{1,0:T(8,128)} %sig_ref.1), channel_id=1, source_target_pairs={{0,1},{1,0},{2,3},{3,2},{4,5},{5,4},{6,7},{7,6},{8,9},{9,8},{10,11... | collective-permute-start | bytes 196616 | tf_op jit(solution)/shard_map/ppermute | solution.py:45
  1.2 2.6 %collective-permute-start.1 = (f32[32,512]{1,0:T(8,128)}, f32[32,512]{1,0:T(8,128)S(1)}, u32[]{:S(2)}, u32[]{:S(2)}) collective-permute-start(f32[32,512]{1,0:T(8,128)} %sig_ref.1), channel_id=1, source_target_pairs={{1,2},{2,1},{5,6},{6,5},{9,10},{10,9},{13,14},{14,13},{17,18},{18,... | collective-permute-start | bytes 196616 | tf_op jit(solution)/shard_map/ppermute | solution.py:45
  3.7 0.8 %pad_maximum_fusion.1.small_ref = f32[25,64]{1,0:T(8,128)S(1)} fusion(f32[6,64]{1,0:T(8,128)} %param.10, f32[1,64]{1,0:T(1,128)} %bitcast.3, f32[9,64]{1,0:T(8,128)} %param.11, f32[9,64]{1,0:T(8,128)} %bitcast.2), kind=kLoop, calls=%fused_computation.3 | loop fusion | flops 4800 | bytes 12800 | tf_op jit(solution)/shard_map/concatenate | solution.py:386
  4.5 0.2 encoder_weights.1.enc_ref
  4.7 0.0 copy-done
  4.7 0.0 copy-done.1
  4.7 1.6 %own.1 = (f32[2,256,128]{2,1,0:T(8,128)S(1)}, f32[2,256,128]{2,1,0:T(8,128)S(1)}, f32[4,256,128]{2,1,0:T(8,128)S(1)}) custom-call(f32[32,512]{1,0:T(8,128)S(1)} %copy-done, f32[25,64]{1,0:T(8,128)S(1)} %pad_maximum_fusion.1.small_ref, f32[6,6,64,64]{3,2,1,0:T(8,128)S(1)} %copy-done.1, bf16[8,2,256,256]{3,2,1,0:T(8,128)(2,1)S(1)} %encoder_weights.1.enc_ref), custom_call_target="tpu_custom_call" | custom-call | flops 1000000000 | bytes 2000000 | tf_op jit(solution)/shard_map/own/pallas_call | solution.py:407
  6.3 0.0 collective-permute-done
  6.3 0.0 collective-permute-done.1
  6.4 1.9 %collective-permute-start.2 = (f32[64,256]{1,0:T(8,128)S(1)}, f32[64,256]{1,0:T(8,128)S(1)}, u32[]{:S(2)}, u32[]{:S(2)}) collective-permute-start(f32[64,256]{1,0:T(8,128)S(1)} %slice.20), channel_id=1, source_target_pairs={{0,4},{4,8},{8,12},{12,16},{16,20},{20,24},{24,28},{28,0},{1,5},{5... | collective-permute-start | bytes 196616 | tf_op jit(solution)/shard_map/ppermute | solution.py:37
  8.3 7.7 %later.1 = (f32[192,128]{1,0:T(8,128)S(1)}, f32[11,16,128]{2,1,0:T(8,128)S(1)}, f32[10,32,128]{2,1,0:T(8,128)S(1)}, bf16[6,2,256,256]{3,2,1,0:T(8,128)(2,1)S(1)}, bf16[5,256,256]{2,1,0:T(8,128)(2,1)S(1)}) custom-call(f32[64,512]{1,0:T(8,128)S(1)} %pad_maximum_fusion.s_ref, f32[25,64]{1,0:T(8,128)S(1)} %pad_maximum_fusion.1.small_ref, ...), custom_call_target="tpu_custom_call" | custom-call | flops 7000000000 | bytes 8000000 | tf_op jit(solution)/shard_map/later/pallas_call | solution.py:427
  16.0 0.0 collective-permute-done.2.hist_ref
  16.0 4.4 %earlier.1 = (f32[32,512]{1,0:T(8,128)}, f32[2,4]{1,0:T(2,128)}) custom-call(f32[64,512]{1,0:T(8,128)S(1)} %pad_maximum_fusion.s_ref, f32[64,256]{1,0:T(8,128)S(1)} %collective-permute-done.2.hist_ref, f32[25,64]{1,0:T(8,128)S(1)} %pad_maximum_fusion.1.small_ref, bf16[8,2,256,256]{3,2,1,0:T(8,128)(2,1)S(1)} %encoder_weights.1.enc_ref, ...), custom_call_target="tpu_custom_call" | custom-call | flops 2000000000 | bytes 8000000 | tf_op jit(solution)/shard_map/earlier/pallas_call | solution.py:443
  (3 shorter events, 0.0 us)
Async XLA Ops:
  0.6 4.0 %copy-start = (f32[32,512]{1,0:T(8,128)S(1)}, f32[32,512]{1,0:T(8,128)}, u32[]{:S(2)}) copy-start(f32[32,512]{1,0:T(8,128)} %sig_ref.1) | copy-start | bytes 196612
  0.6 4.0 %copy-start.1 = (f32[6,6,64,64]{3,2,1,0:T(8,128)S(1)}, f32[6,6,64,64]{3,2,1,0:T(8,128)}, u32[]{:S(2)}) copy-start(f32[6,6,64,64]{3,2,1,0:T(8,128)} %dw_ref.3) | copy-start | bytes 1769476
  0.7 5.7 %collective-permute-start = (f32[32,512]{1,0:T(8,128)}, f32[32,512]{1,0:T(8,128)S(1)}, u32[]{:S(2)}, u32[]{:S(2)}) collective-permute-start(f32[32,512]{1,0:T(8,128)} %sig_ref.1), channel_id=1, source_target_pairs={{0,1},{1,0},{2,3},{3,2},{4,5},{5,4},{6,7},{7,6},{8,9},{9,8},{10,11... | collective-permute-start | bytes 196616 | tf_op jit(solution)/shard_map/ppermute | solution.py:45
  1.2 5.2 %collective-permute-start.1 = (f32[32,512]{1,0:T(8,128)}, f32[32,512]{1,0:T(8,128)S(1)}, u32[]{:S(2)}, u32[]{:S(2)}) collective-permute-start(f32[32,512]{1,0:T(8,128)} %sig_ref.1), channel_id=1, source_target_pairs={{1,2},{2,1},{5,6},{6,5},{9,10},{10,9},{13,14},{14,13},{17,18},{18,... | collective-permute-start | bytes 196616 | tf_op jit(solution)/shard_map/ppermute | solution.py:45
  6.4 9.6 %collective-permute-start.2 = (f32[64,256]{1,0:T(8,128)S(1)}, f32[64,256]{1,0:T(8,128)S(1)}, u32[]{:S(2)}, u32[]{:S(2)}) collective-permute-start(f32[64,256]{1,0:T(8,128)S(1)} %slice.20), channel_id=1, source_target_pairs={{0,4},{4,8},{8,12},{12,16},{16,20},{20,24},{24,28},{28,0},{1,5},{5... | collective-permute-start | bytes 196616 | tf_op jit(solution)/shard_map/ppermute | solution.py:37

commit v6 on v5

--- a/solution.py
+++ b/solution.py
@@ -132,7 +132,8 @@
         kept(layer, i, value, r)
 
     def scale_of(layer, i):
-        return None if mask is None else mask[layer, i : i + 1, :]
+        c = layer - LAYERS + 2 * i
+        return None if mask is None or 0 <= c < CB - 1 else mask[layer, i : i + 1, :]
 
     def chunks(pairs, begin, end):
         units = [(i, r) for i in pairs for r in range(begin, end, CHUNK)]

time: 20.5 us -> 20.3 us (level)
    pallas_call x1, Pallas kernels: 7.67 us -> 7.47 us  [on_device(): pl.pallas_call(later, out_shape=(jax.ShapeDtypeStruct((LATER[LAYERS][1] -...]
where the time goes in v6:
time: 20.3 us; the launch traced here: 20.1 us
  Pallas kernels  13.6 us (67%)
  starting transfers between devices  5 us (25%)
  other arithmetic  0.78 us (4%)
  between operations  0.74 us (4%)
    pallas_call x1, Pallas kernels, on_device(): pl.pallas_call(later, out_shape=(jax.ShapeDtypeStruct((LATER[LAYERS][1] -...  7.47 us
    pallas_call x1, Pallas kernels, on_device(): pl.pallas_call(earlier, out_shape=(jax.ShapeDtypeStruct((2 * CB, 2 * HB),...  4.34 us
    ppermute x2, starting transfers between devices, exchange(): lax.ppermute(block, ('tm', 'fiber'), [p for i, j in swaps for p in ((i, j...  3.08 us
    ppermute x1, starting transfers between devices, from_behind(): lax.ppermute(block, axis, [(i, (i + 1) % count) for i in range(count)])  1.92 us
    pallas_call x1, Pallas kernels, on_device(): pl.pallas_call(own, out_shape=tuple((jax.ShapeDtypeStruct((len(handed(lay...  1.63 us
    concatenate x1, other arithmetic, on_device(): jnp.concatenate([encode_weight.T, decode_weight, encode_bias.reshape(1, F...  0.76 us
  transfers between devices with their start and end apart: 3, of which 0 were waited for; matrix products, arithmetic and copies ran while one was open for 4% of the time, Pallas kernels for 46%

profile of v6, /device:TPU:0, one launch (start us, length us, event | category | flops | bytes accessed | tf_op | source)
XLA Modules:
  0.0 20.1 jit_solution(8491578905118572796)
XLA Ops:
  0.6 0.0 copy-start
  0.6 0.0 copy-start.1
  0.7 0.5 %collective-permute-start = (f32[32,512]{1,0:T(8,128)}, f32[32,512]{1,0:T(8,128)S(1)}, u32[]{:S(2)}, u32[]{:S(2)}) collective-permute-start(f32[32,512]{1,0:T(8,128)} %sig_ref.1), channel_id=1, source_target_pairs={{0,1},{1,0},{2,3},{3,2},{4,5},{5,4},{6,7},{7,6},{8,9},{9,8},{10,11... | collective-permute-start | bytes 196616 | tf_op jit(solution)/shard_map/ppermute | solution.py:45
  1.2 2.6 %collective-permute-start.1 = (f32[32,512]{1,0:T(8,128)}, f32[32,512]{1,0:T(8,128)S(1)}, u32[]{:S(2)}, u32[]{:S(2)}) collective-permute-start(f32[32,512]{1,0:T(8,128)} %sig_ref.1), channel_id=1, source_target_pairs={{1,2},{2,1},{5,6},{6,5},{9,10},{10,9},{13,14},{14,13},{17,18},{18,... | collective-permute-start | bytes 196616 | tf_op jit(solution)/shard_map/ppermute | solution.py:45
  3.7 0.8 %pad_maximum_fusion.1.small_ref = f32[25,64]{1,0:T(8,128)S(1)} fusion(f32[6,64]{1,0:T(8,128)} %param.10, f32[1,64]{1,0:T(1,128)} %bitcast.3, f32[9,64]{1,0:T(8,128)} %param.11, f32[9,64]{1,0:T(8,128)} %bitcast.2), kind=kLoop, calls=%fused_computation.3 | loop fusion | flops 4800 | bytes 12800 | tf_op jit(solution)/shard_map/concatenate | solution.py:387
  4.5 0.2 encoder_weights.1.enc_ref
  4.7 0.0 copy-done
  4.7 0.0 copy-done.1
  4.7 1.6 %own.1 = (f32[2,256,128]{2,1,0:T(8,128)S(1)}, f32[2,256,128]{2,1,0:T(8,128)S(1)}, f32[4,256,128]{2,1,0:T(8,128)S(1)}) custom-call(f32[32,512]{1,0:T(8,128)S(1)} %copy-done, f32[25,64]{1,0:T(8,128)S(1)} %pad_maximum_fusion.1.small_ref, f32[6,6,64,64]{3,2,1,0:T(8,128)S(1)} %copy-done.1, bf16[8,2,256,256]{3,2,1,0:T(8,128)(2,1)S(1)} %encoder_weights.1.enc_ref), custom_call_target="tpu_custom_call" | custom-call | flops 1000000000 | bytes 2000000 | tf_op jit(solution)/shard_map/own/pallas_call | solution.py:408
  6.3 0.0 collective-permute-done
  6.3 0.0 collective-permute-done.1
  6.4 1.9 %collective-permute-start.2 = (f32[64,256]{1,0:T(8,128)S(1)}, f32[64,256]{1,0:T(8,128)S(1)}, u32[]{:S(2)}, u32[]{:S(2)}) collective-permute-start(f32[64,256]{1,0:T(8,128)S(1)} %slice.20), channel_id=1, source_target_pairs={{0,4},{4,8},{8,12},{12,16},{16,20},{20,24},{24,28},{28,0},{1,5},{5... | collective-permute-start | bytes 196616 | tf_op jit(solution)/shard_map/ppermute | solution.py:37
  8.3 7.5 %later.1 = (f32[192,128]{1,0:T(8,128)S(1)}, f32[11,16,128]{2,1,0:T(8,128)S(1)}, f32[10,32,128]{2,1,0:T(8,128)S(1)}, bf16[6,2,256,256]{3,2,1,0:T(8,128)(2,1)S(1)}, bf16[5,256,256]{2,1,0:T(8,128)(2,1)S(1)}) custom-call(f32[64,512]{1,0:T(8,128)S(1)} %pad_maximum_fusion.s_ref, f32[25,64]{1,0:T(8,128)S(1)} %pad_maximum_fusion.1.small_ref, ...), custom_call_target="tpu_custom_call" | custom-call | flops 7000000000 | bytes 8000000 | tf_op jit(solution)/shard_map/later/pallas_call | solution.py:428
  15.8 0.0 collective-permute-done.2.hist_ref
  15.8 4.3 %earlier.1 = (f32[32,512]{1,0:T(8,128)}, f32[2,4]{1,0:T(2,128)}) custom-call(f32[64,512]{1,0:T(8,128)S(1)} %pad_maximum_fusion.s_ref, f32[64,256]{1,0:T(8,128)S(1)} %collective-permute-done.2.hist_ref, f32[25,64]{1,0:T(8,128)S(1)} %pad_maximum_fusion.1.small_ref, bf16[8,2,256,256]{3,2,1,0:T(8,128)(2,1)S(1)} %encoder_weights.1.enc_ref, ...), custom_call_target="tpu_custom_call" | custom-call | flops 2000000000 | bytes 8000000 | tf_op jit(solution)/shard_map/earlier/pallas_call | solution.py:444
  (3 shorter events, 0.0 us)
Async XLA Ops:
  0.6 4.0 %copy-start = (f32[32,512]{1,0:T(8,128)S(1)}, f32[32,512]{1,0:T(8,128)}, u32[]{:S(2)}) copy-start(f32[32,512]{1,0:T(8,128)} %sig_ref.1) | copy-start | bytes 196612
  0.6 4.0 %copy-start.1 = (f32[6,6,64,64]{3,2,1,0:T(8,128)S(1)}, f32[6,6,64,64]{3,2,1,0:T(8,128)}, u32[]{:S(2)}) copy-start(f32[6,6,64,64]{3,2,1,0:T(8,128)} %dw_ref.3) | copy-start | bytes 1769476
  0.7 5.7 %collective-permute-start = (f32[32,512]{1,0:T(8,128)}, f32[32,512]{1,0:T(8,128)S(1)}, u32[]{:S(2)}, u32[]{:S(2)}) collective-permute-start(f32[32,512]{1,0:T(8,128)} %sig_ref.1), channel_id=1, source_target_pairs={{0,1},{1,0},{2,3},{3,2},{4,5},{5,4},{6,7},{7,6},{8,9},{9,8},{10,11... | collective-permute-start | bytes 196616 | tf_op jit(solution)/shard_map/ppermute | solution.py:45
  1.2 5.2 %collective-permute-start.1 = (f32[32,512]{1,0:T(8,128)}, f32[32,512]{1,0:T(8,128)S(1)}, u32[]{:S(2)}, u32[]{:S(2)}) collective-permute-start(f32[32,512]{1,0:T(8,128)} %sig_ref.1), channel_id=1, source_target_pairs={{1,2},{2,1},{5,6},{6,5},{9,10},{10,9},{13,14},{14,13},{17,18},{18,... | collective-permute-start | bytes 196616 | tf_op jit(solution)/shard_map/ppermute | solution.py:45
  6.4 9.4 %collective-permute-start.2 = (f32[64,256]{1,0:T(8,128)S(1)}, f32[64,256]{1,0:T(8,128)S(1)}, u32[]{:S(2)}, u32[]{:S(2)}) collective-permute-start(f32[64,256]{1,0:T(8,128)S(1)} %slice.20), channel_id=1, source_target_pairs={{0,4},{4,8},{8,12},{12,16},{16,20},{20,24},{24,28},{28,0},{1,5},{5... | collective-permute-start | bytes 196616 | tf_op jit(solution)/shard_map/ppermute | solution.py:37
